TPU v7x, 256 devices: a whole 4x4x8 slice. The times are simulated.
256 devices in a mesh: dp: 2 (over z_lo), bricks: 128 (over z_hi, x, y, core).
Axes of the slice: x: 4, y: 4, z: 8 (z_hi: 4, z_lo: 2; z = z_hi * 2 + z_lo), core: 2. Of those that a mesh axis runs over, the one named last changes fastest.
Arguments:
- features: bfloat16 [2, 256, 512, 256], P('dp', 'bricks'), may hold values from -6 to 6
- active: int32 [2, 256, 512], P('dp', 'bricks'), may hold values from 0 to 1, as said below
- neighbours: int32 [2, 256, 27], P('dp', 'bricks'), may hold values from -1 to 255, as said below
- cond: bfloat16 [2, 256, 256], P('dp', 'bricks'), may hold values from -6 to 6
- gamma: float32 [256], replicated, may hold values from 0.1 to 1.9
- beta: float32 [256], replicated, may hold values from -3 to 3
- weight: bfloat16 [27, 256, 256], replicated, may hold values from -0.109375 to 0.109375
- cotangent: bfloat16 [2, 256, 512, 256], P('dp', 'bricks'), may hold values from -6 to 6
Outputs:
- output: bfloat16 [2, 256, 512, 256], P('dp', 'bricks')
- feature_grad: bfloat16 [2, 256, 512, 256], P('dp', 'bricks')
- weight_grad: float32 [1769472], P(('dp', 'bricks'))
Inputs may be any that keep to these rules, and one draw needn't show every extreme that they name: Active voxels lie only in bricks that are present; a present brick's voxels are active at one of three densities; absent bricks have no active voxels. `neighbours`: bricks form a column two bricks wide and high, 64 layers long, four slots a layer in a drawn order; an entry is the global slot index of the present brick one step away in that direction, -1 where there is none; entry 13 is the brick itself or -1 if it is absent; the relation is symmetric under reversing the direction; every neighbour's slot lies on a device whose bricks index differs by at most 3, and that distance is reached.
All inputs are finite; a program needn't handle non-finite values.
Results may differ from a plain program's by a relative error of at most 0.0033.
Values may be sent and summed in bfloat16 or wider, within the bound.
A program may use at most 128 MiB of HBM per device.

v0:
```python
import jax
import jax.numpy as jnp
from jax import lax
from jax.sharding import PartitionSpec as P

GROUPS = 32
BRICK = 8
REACH = 3


EPSILON = 1e-05


def passed_along(block, axis, distance):
    devices = range(lax.axis_size(axis))
    route = [(i - distance, i) for i in devices if i - distance in devices]
    return lax.ppermute(block, axis, route)


def layer_span(step, width):
    if step == -1:
        return slice(width - 1, width)
    if step == 1:
        return slice(0, 1)
    return slice(0, width)


def brick_cut(block, step_x, step_y, step_z):
    width = block.shape[0]
    return block[layer_span(step_x, width), layer_span(step_y, width), layer_span(step_z, width)]


def columns(padded, width):
    patches = []
    for tap_x in range(3):
        for tap_y in range(3):
            for tap_z in range(3):
                window = padded[tap_x : tap_x + width, tap_y : tap_y + width, tap_z : tap_z + width]
                patches.append(window.reshape(width**3, -1))
    return jnp.concatenate(patches, axis=1)


def neighbour_window(table):
    pieces = []
    for offset in range(-REACH, REACH + 1):
        if offset == 0:
            pieces.append(table)
        else:
            pieces.append(passed_along(table, "bricks", -offset))
    return jnp.concatenate(pieces, axis=0)


def assemble(center, window, nbr_row, first_global):
    last_slot = window.shape[0] - 1
    planes = []
    for step_x in (-1, 0, 1):
        lines = []
        for step_y in (-1, 0, 1):
            cells = []
            for step_z in (-1, 0, 1):
                if step_x == 0 and step_y == 0 and (step_z == 0):
                    cells.append(center)
                    continue
                tap_index = (step_x + 1) * 9 + (step_y + 1) * 3 + (step_z + 1)
                target = nbr_row[tap_index]
                local_slot = jnp.clip(target - first_global, 0, last_slot)
                block_piece = lax.dynamic_index_in_dim(window, local_slot, 0, keepdims=False)
                block_piece = jnp.where(target >= 0, block_piece, jnp.zeros_like(block_piece))
                cells.append(brick_cut(block_piece, step_x, step_y, step_z))
            lines.append(jnp.concatenate(cells, axis=2))
        planes.append(jnp.concatenate(lines, axis=1))
    return jnp.concatenate(planes, axis=0)


def on_device(features, active, neighbours, cond, gamma, beta, weight, cotangent):
    inputs = features[0]
    slots, voxels, channels = inputs.shape
    per_group = channels // GROUPS
    mask_f = active[0].astype(jnp.float32)[..., None]
    values = inputs.astype(jnp.float32)

    def group_total(array):
        return jnp.sum(array.reshape(-1, GROUPS, per_group), axis=(0, 2))

    def spread(array):
        return jnp.repeat(array, per_group)

    local_count = jnp.sum(mask_f)
    local_first = group_total(mask_f * values)
    active_count, sum_first = lax.psum((local_count, local_first), "bricks")
    active_count = active_count * per_group
    group_mean = sum_first / active_count
    centred = values - spread(group_mean)
    group_var = lax.psum(group_total(mask_f * centred * centred), "bricks") / active_count
    inv_std = spread(lax.rsqrt(group_var + EPSILON))
    x_hat = (values - spread(group_mean)) * inv_std
    pre_act = x_hat * gamma + beta + cond[0].astype(jnp.float32)[:, None, :]
    sigma = jax.nn.sigmoid(pre_act)
    hidden = (mask_f * pre_act * sigma).astype(jnp.bfloat16)
    masked_cot = active[0].astype(jnp.bfloat16)[..., None] * cotangent[0]
    h_table = hidden.reshape(slots, BRICK, BRICK, BRICK, channels)
    z_table = masked_cot.reshape(slots, BRICK, BRICK, BRICK, channels)
    w_fwd = weight.reshape(27 * channels, channels)
    w_back = jnp.transpose(weight[::-1], (0, 2, 1)).reshape(27 * channels, channels)
    first_global = (lax.axis_index("bricks") - REACH) * slots
    h_window = neighbour_window(h_table)
    z_window = neighbour_window(z_table)
    conv_parts = []
    grad_parts = []
    w_grad = jnp.zeros((27 * channels, channels), jnp.float32)
    for slot in range(slots):
        nbr_row = neighbours[0, slot]
        patches = columns(assemble(h_table[slot], h_window, nbr_row, first_global), BRICK)
        conv_parts.append(jnp.dot(patches, w_fwd, preferred_element_type=jnp.float32))
        back_patches = columns(assemble(z_table[slot], z_window, nbr_row, first_global), BRICK)
        grad_parts.append(jnp.dot(back_patches, w_back, preferred_element_type=jnp.float32))
        w_grad = w_grad + lax.dot_general(
            patches, masked_cot[slot], (((0,), (0,)), ((), ())), preferred_element_type=jnp.float32
        )
    conv_out = jnp.stack(conv_parts)
    hidden_grad = jnp.stack(grad_parts)
    output = (mask_f * (values + conv_out)).astype(jnp.bfloat16)
    scaled_grad = gamma * mask_f * hidden_grad * sigma * (1.0 + pre_act * (1.0 - sigma))
    grad_sum, cross_sum = lax.psum(
        (group_total(scaled_grad), group_total(scaled_grad * x_hat)), "bricks"
    )
    grad_mean = spread(grad_sum / active_count)
    cross_mean = spread(cross_sum / active_count)
    feature_grad = mask_f * (
        inv_std * (scaled_grad - grad_mean - x_hat * cross_mean) + cotangent[0].astype(jnp.float32)
    )
    flat_grad = w_grad.reshape(-1)
    weight_grad = lax.psum_scatter(flat_grad, ("dp", "bricks"), scatter_dimension=0, tiled=True)
    return (output[None], feature_grad.astype(jnp.bfloat16)[None], weight_grad)


def solution(mesh):
    in_specs = (
        P("dp", "bricks", None, None),
        P("dp", "bricks", None),
        P("dp", "bricks", None),
        P("dp", "bricks", None),
        P(),
        P(),
        P(),
        P("dp", "bricks", None, None),
    )
    out_specs = (P("dp", "bricks", None, None), P("dp", "bricks", None, None), P(("dp", "bricks")))
    return jax.shard_map(
        on_device, mesh=mesh, in_specs=in_specs, out_specs=out_specs, check_vma=False
    )
```

profile of v0, /device:TPU:128, one launch (start us, length us, event | category | flops | bytes accessed | tf_op | source)
XLA Modules:
  0.0 1384.5 jit_solution(12672699699441867288)
XLA Ops:
  8.1 2.0 broadcast_multiply_fusion
  10.2 1.9 collective-permute-start.8
  12.1 3.5 collective-permute-start.7
  19.0 368.9 %all-reduce.2 = (f32[32]{0:T(128)S(1)}, f32[]{:T(128)}) all-reduce(f32[32]{0:T(128)S(1)} %reduce_sum.59, f32[]{:T(128)} %convert_reduce_fusion), channel_id=1, replica_groups=mesh['dp'=2,'bricks'=128] {'bricks'}, use_global_device_ids=true, to_apply=%region_2.0 | all-reduce | flops 33 | bytes 264 | tf_op jit(solution)/shard_map/psum | solution.py:90
  390.2 355.4 %psum.37 = f32[32]{0:T(128)S(1)} all-reduce(f32[32]{0:T(128)S(1)} %reduce_sum.66), channel_id=1, replica_groups=mesh['dp'=2,'bricks'=128] {'bricks'}, use_global_device_ids=true, to_apply=%region_7.8 | all-reduce | flops 32 | bytes 256 | tf_op jit(solution)/shard_map/psum | solution.py:94
  745.8 2.4 multiply_convert_fusion.1
  748.2 2.2 collective-permute-start.2
  750.5 1.9 collective-permute-start.1
  752.4 1.9 collective-permute-start
  822.4 4.4 copy.12
  826.9 2.0 rev.3
  830.0 1.9 collective-permute-start.6
  833.0 10.2 collective-permute-start.4
  844.4 2.9 collective-permute-start.3
  848.9 2.5 collective-permute-done.6
  851.4 5.1 collective-permute-start.11
  856.6 58.9 %collective-permute-done.3 = bf16[2,8,8,8,256]{4,3,2,1,0:T(8,128)(2,1)S(1)} collective-permute-done((bf16[2,8,8,8,256]{4,3,2,1,0:T(8,128)(2,1)}, bf16[2,8,8,8,256]{4,3,2,1,0:T(8,128)(2,1)S(1)}, u32[]{:S(2)}, u32[]{:S(2)}) %collective-permute-start.3) | collective-permute-done | bytes 524320 | tf_op jit(solution)/shard_map/ppermute | solution.py:17
  915.4 1.9 collective-permute-start.10
  917.4 1.9 collective-permute-start.5
  919.4 10.7 collective-permute-start.9
  932.5 23.8 %collective-permute-done.5 = bf16[2,8,8,8,256]{4,3,2,1,0:T(8,128)(2,1)S(1)} collective-permute-done((bf16[2,8,8,8,256]{4,3,2,1,0:T(8,128)(2,1)}, bf16[2,8,8,8,256]{4,3,2,1,0:T(8,128)(2,1)S(1)}, u32[]{:S(2)}, u32[]{:S(2)}) %collective-permute-start.5) | collective-permute-done | bytes 524320 | tf_op jit(solution)/shard_map/ppermute | solution.py:17
  956.4 5.6 collective-permute-done.9
  976.0 2.0 fusion.51
  978.4 2.0 fusion.52
  988.7 2.0 fusion.16
  992.0 2.9 copy-done.2
  994.9 4.9 fusion
  999.8 9.5 copy.13
  1010.0 352.3 %all-reduce.1 = (f32[32]{0:T(128)S(1)}, f32[32]{0:T(128)S(1)}) all-reduce(f32[32]{0:T(128)S(1)} %reduce_sum.85, f32[32]{0:T(128)S(1)} %reduce_sum.82), channel_id=1, replica_groups=mesh['dp'=2,'bricks'=128] {'bricks'}, use_global_device_ids=true, to_apply=%region_13.14 | all-reduce | flops 64 | bytes 512 | tf_op jit(solution)/shard_map/psum | solution.py:124
  1362.7 6.2 convolution_bitcast_fusion.1
  1368.9 5.0 convolution_bitcast_fusion
  1373.9 1.9 fusion.11
  (334 shorter events, 41.3 us)
Async XLA Ops:
  7.2 747.2 %copy-start.4 = (bf16[1,2,512,256]{3,2,1,0:T(8,128)(2,1)S(1)}, bf16[1,2,512,256]{3,2,1,0:T(8,128)(2,1)}, u32[]{:S(2)}) copy-start(bf16[1,2,512,256]{3,2,1,0:T(8,128)(2,1)} %param.15) | copy-start | bytes 1572868
  7.2 748.2 %copy-start.8 = (s32[1,2,27]{2,1,0:T(2,128)S(1)}, s32[1,2,27]{2,1,0:T(2,128)}, u32[]{:S(2)}) copy-start(s32[1,2,27]{2,1,0:T(2,128)} %param.10) | copy-start | bytes 652
  7.2 1368.6 %all-reduce.5.cloned.1.call-start = ((), (), s32[]{:S(2)}) async-start(), calls=%async_computation | async-start | bytes 14155776
  8.1 737.6 %copy-start.11 = (bf16[2,8,8,8]{3,2,1,0:T(8,128)(2,1)}, bf16[2,8,8,8]{3,2,1,0:T(8,128)(2,1)S(1)}, u32[]{:S(2)}) copy-start(bf16[2,8,8,8]{3,2,1,0:T(8,128)(2,1)S(1)} %convert_element_type.99) | copy-start | bytes 6148
  10.2 921.0 %collective-permute-start.8 = (bf16[2,8,8,8,256]{4,3,2,1,0:T(8,128)(2,1)}, bf16[2,8,8,8,256]{4,3,2,1,0:T(8,128)(2,1)}, u32[]{:S(2)}, u32[]{:S(2)}) collective-permute-start(bf16[2,8,8,8,256]{4,3,2,1,0:T(8,128)(2,1)} %broadcast_multiply_fusion), channel_id=1, source_target_pairs={{0,1},{1,2},{2,3},{3,4},{4,5},{5,6},{6,7},{7,8},{8,9},{9,10},{10,1... | collective-permute-start | bytes 1572872 | tf_op jit(solution)/shard_map/ppermute | solution.py:17
  12.1 907.3 %collective-permute-start.7 = (bf16[2,8,8,8,256]{4,3,2,1,0:T(8,128)(2,1)}, bf16[2,8,8,8,256]{4,3,2,1,0:T(8,128)(2,1)}, u32[]{:S(2)}, u32[]{:S(2)}) collective-permute-start(bf16[2,8,8,8,256]{4,3,2,1,0:T(8,128)(2,1)} %broadcast_multiply_fusion), channel_id=1, source_target_pairs={{0,2},{1,3},{2,4},{3,5},{4,6},{5,7},{6,8},{7,9},{8,10},{9,11},{10,... | collective-permute-start | bytes 1572872 | tf_op jit(solution)/shard_map/ppermute | solution.py:17
  745.8 76.6 %copy-start.9 = (f32[2,8,8,8]{3,2,1,0:T(8,128)}, f32[2,8,8,8]{3,2,1,0:T(8,128)S(1)}, u32[]{:S(2)}) copy-start(f32[2,8,8,8]{3,2,1,0:T(8,128)S(1)} %convert_element_type.88) | copy-start | bytes 12292
  748.2 96.2 %collective-permute-start.2 = (bf16[2,8,8,8,256]{4,3,2,1,0:T(8,128)(2,1)}, bf16[2,8,8,8,256]{4,3,2,1,0:T(8,128)(2,1)}, u32[]{:S(2)}, u32[]{:S(2)}) collective-permute-start(bf16[2,8,8,8,256]{4,3,2,1,0:T(8,128)(2,1)} %multiply_convert_fusion.1), channel_id=1, source_target_pairs={{0,1},{1,2},{2,3},{3,4},{4,5},{5,6},{6,7},{7,8},{8,9},{9,10},{10,1... | collective-permute-start | bytes 1572872 | tf_op jit(solution)/shard_map/ppermute | solution.py:17
  750.5 82.6 %collective-permute-start.1 = (bf16[2,8,8,8,256]{4,3,2,1,0:T(8,128)(2,1)}, bf16[2,8,8,8,256]{4,3,2,1,0:T(8,128)(2,1)}, u32[]{:S(2)}, u32[]{:S(2)}) collective-permute-start(bf16[2,8,8,8,256]{4,3,2,1,0:T(8,128)(2,1)} %multiply_convert_fusion.1), channel_id=1, source_target_pairs={{0,2},{1,3},{2,4},{3,5},{4,6},{5,7},{6,8},{7,9},{8,10},{9,11},{10,... | collective-permute-start | bytes 1572872 | tf_op jit(solution)/shard_map/ppermute | solution.py:17
  752.4 77.6 %collective-permute-start = (bf16[2,8,8,8,256]{4,3,2,1,0:T(8,128)(2,1)}, bf16[2,8,8,8,256]{4,3,2,1,0:T(8,128)(2,1)}, u32[]{:S(2)}, u32[]{:S(2)}) collective-permute-start(bf16[2,8,8,8,256]{4,3,2,1,0:T(8,128)(2,1)} %multiply_convert_fusion.1), channel_id=1, source_target_pairs={{0,3},{1,4},{2,5},{3,6},{4,7},{5,8},{6,9},{7,10},{8,11},{9,12},{10... | collective-permute-start | bytes 1572872 | tf_op jit(solution)/shard_map/ppermute | solution.py:17
  828.9 19.5 %copy-start = (bf16[1,2,512,256]{3,2,1,0:T(8,128)(2,1)S(1)}, bf16[1,2,512,256]{3,2,1,0:T(8,128)(2,1)}, u32[]{:S(2)}) copy-start(bf16[1,2,512,256]{3,2,1,0:T(8,128)(2,1)} %param.8) | copy-start | bytes 1572868
  828.9 19.5 %copy-start.10 = (f32[2,8,8,8]{3,2,1,0:T(8,128)S(1)}, f32[2,8,8,8]{3,2,1,0:T(8,128)}, u32[]{:S(2)}) copy-start(f32[2,8,8,8]{3,2,1,0:T(8,128)} %copy-done.9) | copy-start | bytes 12292
  828.9 19.5 %copy-start.13 = (f32[256]{0:T(256)S(1)}, f32[256]{0:T(256)}, u32[]{:S(2)}) copy-start(f32[256]{0:T(256)} %param.13) | copy-start | bytes 3076
  828.9 19.5 %copy-start.14 = (f32[256]{0:T(256)S(1)}, f32[256]{0:T(256)}, u32[]{:S(2)}) copy-start(f32[256]{0:T(256)} %param.12) | copy-start | bytes 3076
  830.0 21.4 %collective-permute-start.6 = (bf16[2,8,8,8,256]{4,3,2,1,0:T(8,128)(2,1)}, bf16[2,8,8,8,256]{4,3,2,1,0:T(8,128)(2,1)S(1)}, u32[]{:S(2)}, u32[]{:S(2)}) collective-permute-start(bf16[2,8,8,8,256]{4,3,2,1,0:T(8,128)(2,1)} %broadcast_multiply_fusion), channel_id=1, source_target_pairs={{0,3},{1,4},{2,5},{3,6},{4,7},{5,8},{6,9},{7,10},{8,11},{9,12},{10... | collective-permute-start | bytes 1572872 | tf_op jit(solution)/shard_map/ppermute | solution.py:17
  833.0 84.4 %collective-permute-start.4 = (bf16[2,8,8,8,256]{4,3,2,1,0:T(8,128)(2,1)}, bf16[2,8,8,8,256]{4,3,2,1,0:T(8,128)(2,1)S(1)}, u32[]{:S(2)}, u32[]{:S(2)}) collective-permute-start(bf16[2,8,8,8,256]{4,3,2,1,0:T(8,128)(2,1)} %multiply_convert_fusion.1), channel_id=1, source_target_pairs={{2,0},{3,1},{4,2},{5,3},{6,4},{7,5},{8,6},{9,7},{10,8},{11,9},{12,... | collective-permute-start | bytes 1572872 | tf_op jit(solution)/shard_map/ppermute | solution.py:17
  844.4 87.9 %copy-start.5 = (bf16[1,2,512,256]{3,2,1,0:T(8,128)(2,1)S(1)}, bf16[1,2,512,256]{3,2,1,0:T(8,128)(2,1)}, u32[]{:S(2)}) copy-start(bf16[1,2,512,256]{3,2,1,0:T(8,128)(2,1)} %param.15) | copy-start | bytes 1572868
  844.4 87.9 %copy-start.12 = (bf16[2,8,8,8]{3,2,1,0:T(8,128)(2,1)S(1)}, bf16[2,8,8,8]{3,2,1,0:T(8,128)(2,1)}, u32[]{:S(2)}) copy-start(bf16[2,8,8,8]{3,2,1,0:T(8,128)(2,1)} %copy-done.11) | copy-start | bytes 6148
  844.4 71.0 %collective-permute-start.3 = (bf16[2,8,8,8,256]{4,3,2,1,0:T(8,128)(2,1)}, bf16[2,8,8,8,256]{4,3,2,1,0:T(8,128)(2,1)S(1)}, u32[]{:S(2)}, u32[]{:S(2)}) collective-permute-start(bf16[2,8,8,8,256]{4,3,2,1,0:T(8,128)(2,1)} %multiply_convert_fusion.1), channel_id=1, source_target_pairs={{1,0},{2,1},{3,2},{4,3},{5,4},{6,5},{7,6},{8,7},{9,8},{10,9},{11,1... | collective-permute-start | bytes 1572872 | tf_op jit(solution)/shard_map/ppermute | solution.py:17
  851.4 110.8 %collective-permute-start.11 = (bf16[2,8,8,8,256]{4,3,2,1,0:T(8,128)(2,1)}, bf16[2,8,8,8,256]{4,3,2,1,0:T(8,128)(2,1)S(1)}, u32[]{:S(2)}, u32[]{:S(2)}) collective-permute-start(bf16[2,8,8,8,256]{4,3,2,1,0:T(8,128)(2,1)} %broadcast_multiply_fusion), channel_id=1, source_target_pairs={{3,0},{4,1},{5,2},{6,3},{7,4},{8,5},{9,6},{10,7},{11,8},{12,9},{13... | collective-permute-start | bytes 1572872 | tf_op jit(solution)/shard_map/ppermute | solution.py:17
  915.4 46.6 %collective-permute-start.10 = (bf16[2,8,8,8,256]{4,3,2,1,0:T(8,128)(2,1)}, bf16[2,8,8,8,256]{4,3,2,1,0:T(8,128)(2,1)S(1)}, u32[]{:S(2)}, u32[]{:S(2)}) collective-permute-start(bf16[2,8,8,8,256]{4,3,2,1,0:T(8,128)(2,1)} %broadcast_multiply_fusion), channel_id=1, source_target_pairs={{2,0},{3,1},{4,2},{5,3},{6,4},{7,5},{8,6},{9,7},{10,8},{11,9},{12,... | collective-permute-start | bytes 1572872 | tf_op jit(solution)/shard_map/ppermute | solution.py:17
  917.4 38.9 %collective-permute-start.5 = (bf16[2,8,8,8,256]{4,3,2,1,0:T(8,128)(2,1)}, bf16[2,8,8,8,256]{4,3,2,1,0:T(8,128)(2,1)S(1)}, u32[]{:S(2)}, u32[]{:S(2)}) collective-permute-start(bf16[2,8,8,8,256]{4,3,2,1,0:T(8,128)(2,1)} %multiply_convert_fusion.1), channel_id=1, source_target_pairs={{3,0},{4,1},{5,2},{6,3},{7,4},{8,5},{9,6},{10,7},{11,8},{12,9},{13... | collective-permute-start | bytes 1572872 | tf_op jit(solution)/shard_map/ppermute | solution.py:17
  919.4 42.6 %collective-permute-start.9 = (bf16[2,8,8,8,256]{4,3,2,1,0:T(8,128)(2,1)}, bf16[2,8,8,8,256]{4,3,2,1,0:T(8,128)(2,1)S(1)}, u32[]{:S(2)}, u32[]{:S(2)}) collective-permute-start(bf16[2,8,8,8,256]{4,3,2,1,0:T(8,128)(2,1)} %broadcast_multiply_fusion), channel_id=1, source_target_pairs={{1,0},{2,1},{3,2},{4,3},{5,4},{6,5},{7,6},{8,7},{9,8},{10,9},{11,1... | collective-permute-start | bytes 1572872 | tf_op jit(solution)/shard_map/ppermute | solution.py:17
  972.9 1.0 copy-start.3
  974.0 2.0 copy-start.7
  988.7 2.9 copy-start.1
  992.0 2.9 copy-start.2
  1362.7 6.2 copy-start.6
Sparse Core Ops, SparseCore 0:
  1009.5 275.3 all-reduce.4
where the time goes:
time: 1390 us; the launch traced here: 1380 us
  blocking collectives  1080 us (78%)
  waiting for transfers between devices  90.8 us (7%)
  between operations  82.4 us (6%)
  starting transfers between devices  46.2 us (3%)
  local copies, waits for them, and re-layouts  40.6 us (3%)
  other arithmetic  25.8 us (2%)
  matrix products  22.1 us (2%)
    psum x1, blocking collectives, on_device(): active_count, sum_first = lax.psum((local_count, local_first), 'bricks')  369 us
    psum x1, blocking collectives, on_device(): lax.psum(group_total(mask_f * centred * centred), 'bricks') / active_count  355 us
    psum x1, blocking collectives, on_device(): lax.psum((group_total(scaled_grad), group_total(scaled_grad * x_hat)), 'b...  352 us
    ppermute x12, waiting for transfers between devices, passed_along(): return lax.ppermute(block, axis, route)  90.8 us
    ppermute x12, starting transfers between devices, passed_along(): return lax.ppermute(block, axis, route)  46.2 us
    unnamed x145, local copies, waits for them, and re-layouts  29 us
  transfers between devices with their start and end apart: 13, of which 4 were waited for; matrix products, arithmetic and copies ran while one was open for 3% of the time, Pallas kernels for 0%

commit v1 on v0

v1 whole, which is shorter than its diff:
```python
import functools

import jax
import jax.numpy as jnp
from jax import lax
from jax.experimental import pallas as pl
from jax.experimental.pallas import tpu as pltpu
from jax.sharding import PartitionSpec as P

MESH = pl.DeviceIdType.MESH
F32 = jnp.float32
BF16 = jnp.bfloat16
EPSILON = 1e-05
BIG = 1e30
LIMIT = 1e29
LAYERS = 64
ROWS = 3456
CUTS = (0, 4, 8, 11, 14)


def moved(index, stride, size, step):
    digit = (index // stride) % size
    return index + ((digit + step) % size - digit) * stride


def block_sum(v):
    return jnp.sum(v.reshape(v.shape[0] // 8, 8, v.shape[1]), axis=0)


def column_sum(v):
    return jnp.sum(v, axis=0, keepdims=True)


def packet(*rows):
    place = lax.broadcasted_iota(jnp.int32, (8, 256), 0)
    out = jnp.zeros((8, 256), F32)
    for i, row in enumerate(rows):
        out = jnp.where(place == i, row, out)
    return out


def pooled(parts):
    count = sum(p[2:3] for p in parts)
    first = sum(p[0:1] for p in parts)
    mean = first / jnp.maximum(count, 1.0)
    second = sum(p[1:2] for p in parts)
    for p in parts:
        apart = p[0:1] / jnp.maximum(p[2:3], 1.0) - mean
        second = second + p[2:3] * apart * apart
    return packet(first, second, count)


def group_sum(row):
    v = jnp.broadcast_to(row, (8, 256))
    lane = lax.broadcasted_iota(jnp.int32, (8, 256), 1)
    for step in (1, 2, 4):
        up = pltpu.roll(v, 256 - step, 1)
        down = pltpu.roll(v, step, 1)
        v = v + jnp.where((lane & step) == 0, up, down)
    return v[0:1]


def kernel(
    feat, cot, act, nbr, cond, gamma_in, beta_in, w_hbm,
    out, fgrad, wgrad,
    fs, zs, face_f, face_z, conds, conds_e, nbv, nbs,
    w_fwd, w_back, hz, zz, zt, wg, part, r1, r2, r3, r4, fin, fin_r,
    acc_f, acc_b, sg_s, outs, grads,
    own, got1, got2, got3, back1, back2, back3,
    w_sem, nb_sem, core_s, core_r, edge_s, edge_r, st_s, st_r, rs1_s, rs1_r, rs2_s, rs2_r, rs3_s, rs3_r, rs4_s, rs4_r,
    fin_s, fin_rs, res_s, res_r,
):
    d = lax.axis_index("dp")
    b = lax.axis_index("bricks")
    c = b % 2
    layer = b // 2
    xm = (b // 8) % 4
    ym = (b // 2) % 4
    hm = b // 32
    other = b + 1 - 2 * c
    after0 = ((layer + 1) % LAYERS) * 2
    before1 = ((layer + LAYERS - 1) % LAYERS) * 2 + 1
    beside = jnp.where(c == 0, (layer + LAYERS - 1) % LAYERS, (layer + 1) % LAYERS) * 2

    def copy(src, dst, ssem, rsem, dev):
        return pltpu.make_async_remote_copy(
            src_ref=src, dst_ref=dst, send_sem=ssem, recv_sem=rsem, device_id=dev, device_id_type=MESH
        )

    w_copy = pltpu.make_async_copy(w_hbm, w_fwd, w_sem)
    w_copy.start()

    barrier = pltpu.get_barrier_semaphore()
    partners = [{"bricks": moved(b, 1, 8, j)} for j in range(1, 8)]
    partners += [{"bricks": moved(b, 8, 4, j)} for j in range(1, 4)]
    partners += [{"bricks": moved(b, 32, 4, j)} for j in range(1, 4)]
    partners += [{"dp": 1 - d, "bricks": b}, {"dp": 1 - d, "bricks": other}]
    partners += [{"bricks": after0}, {"bricks": before1}, {"bricks": beside}, {"bricks": beside + 1}]
    for dev in partners:
        pl.semaphore_signal(barrier, inc=1, device_id=dev, device_id_type=MESH)

    rows = [act[s : s + 1, 128 * j : 128 * j + 128] for s in range(2) for j in range(4)]
    flags = jnp.concatenate(rows, axis=0).astype(F32)
    count = jnp.sum(jnp.sum(flags, axis=1, keepdims=True), axis=0, keepdims=True)
    flags_t = flags.T
    first = jnp.zeros((8, 256), F32)
    for s in range(2):
        for j in range(4):
            at = pl.ds(128 * j, 128)
            m = jnp.broadcast_to(flags_t[:, 4 * s + j : 4 * s + j + 1], (128, 256)) > 0.5
            f = feat[s, at, :].astype(F32)
            z = cot[s, at, :].astype(F32)
            fs[2 * c + s, at, :] = jnp.where(m, f, BIG).astype(BF16)
            zs[2 * c + s, at, :] = jnp.where(m, z, 0.0).astype(BF16)
            first = first + block_sum(jnp.where(m, f, 0.0))
    first = column_sum(first)
    local_mean = first / jnp.maximum(count, 1.0)
    second = jnp.zeros((8, 256), F32)
    for s in range(2):
        for j in range(4):
            f = fs[2 * c + s, pl.ds(128 * j, 128), :].astype(F32)
            apart = jnp.where(f < LIMIT, f - local_mean, 0.0)
            second = second + block_sum(apart * apart)
    second = column_sum(second)
    own[0] = packet(first, second, jnp.broadcast_to(count, (1, 256)))
    nbv[c] = jnp.zeros((8, 128), jnp.int32)
    nbv[c, 0:2, 0:27] = nbr[...]
    for s in range(2):
        conds[2 * c + s] = jnp.broadcast_to(cond[s : s + 1, :].astype(F32), (8, 256))
    pl.semaphore_wait(barrier, len(partners))

    def spread_start(stage, stride, size, boxes, base):
        sent = []
        for j in range(1, size):
            cp = copy(
                own.at[stage], boxes.at[j - 1], st_s.at[base + j - 1], st_r.at[base + j - 1],
                {"bricks": moved(b, stride, size, j)},
            )
            cp.start()
            sent.append(cp)
        return sent

    def spread_end(sent, stage, boxes):
        for cp in sent:
            cp.wait()
        return [own[stage]] + [boxes[j] for j in range(len(sent))]

    sent = spread_start(0, 1, 8, got1, 0)

    mine = pl.ds(2 * c, 2)
    core_copies = [
        copy(r.at[i], r.at[i], core_s.at[k], core_r.at[k], {"bricks": other})
        for k, (r, i) in enumerate(((nbv, c), (zs, mine), (fs, mine), (conds, mine)))
    ]
    for cp in core_copies:
        cp.start()
    edge_copies = []
    for k, (src, dst, up, down) in enumerate((
        (zs, face_z, pl.ds(448, 64), pl.ds(0, 64)),
        (fs, face_f, pl.ds(448, 64), pl.ds(0, 64)),
        (conds, conds_e, pl.ds(0, 8), pl.ds(0, 8)),
    )):
        for way, (at, dev) in enumerate(((up, after0), (down, before1))):
            cp = copy(
                src.at[mine, at], dst.at[mine], edge_s.at[2 * k + way], edge_r.at[k, c], {"bricks": dev}
            )
            cp.start()
            edge_copies.append(cp)

    def edge_wait(k, dst):
        for core in range(2):
            got = dst.at[pl.ds(2 * core, 2)]
            copy(got, got, edge_s.at[2 * k], edge_r.at[k, core], {"bricks": other}).wait_recv()

    for grid in (hz, zz):
        grid[:, 0:16, :] = jnp.zeros((10, 16, 768), BF16)
        grid[:, 272:288, :] = jnp.zeros((10, 16, 768), BF16)
    fs[4] = jnp.full((512, 256), BIG, BF16)
    zs[4] = jnp.zeros((512, 256), BF16)
    face_f[4] = jnp.full((64, 256), BIG, BF16)
    face_z[4] = jnp.zeros((64, 256), BF16)
    conds[4] = jnp.zeros((8, 256), F32)
    conds_e[4] = jnp.zeros((8, 256), F32)
    wg[pl.ds(128 + ROWS, 128), :] = jnp.zeros((128, 256), F32)

    w_copy.wait()

    def turn(g, carry):
        for e in range(3):
            w_back[g, pl.ds(256 * e, 256), :] = w_fwd[8 - g, pl.ds(256 * (2 - e), 256), :].T
        return carry

    lax.fori_loop(0, 9, turn, 0)

    merged = pooled(spread_end(sent, 0, got1))
    own[1] = merged
    sent = spread_start(1, 8, 4, got2, 7)

    core_copies[0].wait()
    nb_copy = pltpu.make_async_copy(nbv, nbs, nb_sem)
    nb_copy.start()
    nb_copy.wait()
    cy, cz, src, src_e = [], [], [], []
    here = []
    for j in range(4):
        def entry(k):
            return nbs[j // 2, j % 2, k]

        low_y = functools.reduce(jnp.maximum, [entry(9 * a + e) for a in range(3) for e in range(3)])
        low_z = functools.reduce(jnp.maximum, [entry(9 * a + 3 * e) for a in range(3) for e in range(3)])
        cy.append(jnp.where(low_y >= 0, 1, 0))
        cz.append(jnp.where(low_z >= 0, 1, 0))
        here.append(entry(13) >= 0)
    for q in range(4):
        qy, qz = q // 2, q % 2
        at, at_e = jnp.int32(4), jnp.int32(4)
        for j in range(4):
            at = jnp.where(here[j] & (cy[j] == qy) & (cz[j] == qz), j, at)
            t = nbs[j // 2, j % 2, 18 * c + 3 * (qy + 1 - cy[j]) + (qz + 1 - cz[j])]
            at_e = jnp.where(t >= 0, t & 3, at_e)
        src.append(at)
        src_e.append(at_e)

    zi = lax.broadcasted_iota(jnp.int32, (128, 256), 0) & 15

    def joined(left, right):
        pair = [v.reshape(8, 8, 256) for v in (left, right)]
        return jnp.concatenate(pair, axis=1).reshape(128, 256)

    def lay(grid, plane, half, v):
        at = pl.ds(16 + 128 * half, 128)
        grid[plane, at, 0:256] = jnp.where(zi == 0, 0.0, pltpu.roll(v, 1, 0)).astype(BF16)
        grid[plane, at, 256:512] = v.astype(BF16)
        grid[plane, at, 512:768] = jnp.where(zi == 15, 0.0, pltpu.roll(v, 127, 0)).astype(BF16)

    edge_plane = 9 * c

    core_copies[1].wait()
    edge_wait(0, face_z)

    def lay_z(x, carry):
        for half in range(2):
            at = pl.ds(pl.multiple_of(64 * x, 64), 64)
            v = joined(*[zs[src[2 * half + e], at, :].astype(F32) for e in range(2)])
            lay(zz, x + 1, half, v)
            zt[:, pl.ds(pl.multiple_of(256 * x + 128 * half, 128), 128)] = v.T.astype(BF16)
        return carry

    lax.fori_loop(0, 8, lay_z, 0)
    for half in range(2):
        lay(zz, edge_plane, half, joined(*[face_z[src_e[2 * half + e]].astype(F32) for e in range(2)]))

    merged = pooled(spread_end(sent, 1, got2))
    own[2] = merged
    sent = spread_start(2, 32, 4, got3, 10)

    def conv(grid, taps, acc, low, high):
        def step(g, carry):
            at = pl.ds(pl.multiple_of((g % 3) * 16, 16), 256)
            lhs = grid[pl.ds(4 * c + g // 3, 4), at, :].reshape(1024, 768)
            acc[...] += jnp.dot(lhs, taps[g], preferred_element_type=F32).reshape(4, 2, 8, 2, 8, 256)
            return carry

        lax.fori_loop(low, high, step, 0)

    acc_f[...] = jnp.zeros(acc_f.shape, F32)
    acc_b[...] = jnp.zeros(acc_b.shape, F32)
    conv(zz, w_back, acc_b, 0, 5)

    merged = pooled(spread_end(sent, 2, got3))
    total = merged[2:3]
    first, second = merged[0:1], merged[1:2]
    total_g = 8.0 * total
    mean = group_sum(first) / total_g
    apart = first / total - mean
    var = group_sum(second + total * apart * apart) / total_g
    inv_std = lax.rsqrt(var + EPSILON)
    gamma = gamma_in[...]
    beta = beta_in[...]
    slope = inv_std * gamma

    for cp in core_copies[2:]:
        cp.wait()
    edge_wait(1, face_f)
    edge_wait(2, conds_e)

    def activation(raw, shift):
        f = raw.astype(F32)
        m = f < LIMIT
        f = jnp.where(m, f, 0.0)
        apart = f - mean
        pre = apart * slope + (beta + shift[0:1])
        sigma = 1.0 / (1.0 + jnp.exp(-pre))
        return m, f, apart, pre, sigma

    def hidden(raw, shift):
        m, _, _, pre, sigma = activation(raw, shift)
        return jnp.where(m, pre * sigma, 0.0)

    def lay_h(x, carry):
        for half in range(2):
            at = pl.ds(pl.multiple_of(64 * x, 64), 64)
            slots = [src[2 * half + e] for e in range(2)]
            lay(hz, x + 1, half, joined(*[hidden(fs[j, at, :], conds[j]) for j in slots]))
        return carry

    lax.fori_loop(0, 8, lay_h, 0)
    for half in range(2):
        slots = [src_e[2 * half + e] for e in range(2)]
        lay(hz, edge_plane, half, joined(*[hidden(face_f[j], conds_e[j]) for j in slots]))

    def taps(low, high):
        def step(i, carry):
            t = 13 * c + i
            at = pl.ds(pl.multiple_of((t // 3) % 3 * 16, 16), 256)
            lanes = pl.ds(pl.multiple_of(t % 3 * 256, 256), 256)
            rhs = hz[pl.ds(t // 9, 8), at, lanes].reshape(2048, 256)
            made = jnp.dot(zt[...], rhs, preferred_element_type=F32)
            wg[pl.ds(pl.multiple_of(128 * (1 - c) + 256 * i, 128), 256), :] = made.T
            return carry

        lax.fori_loop(low, high, step, 0)

    way = ((8, 2), (2, 8))
    place = ((xm, ym), (ym, xm))

    def deal(h):
        def step(x, carry):
            base = pl.multiple_of(128 + 864 * h + 216 * x, 8)
            for y in range(4):
                low = 54 * y // 8 * 8
                v = wg[pl.ds(base + low, 64), :][54 * y - low : 54 * y - low + 56]
                part[0, x, h, y] = v[:, 0:128]
                part[1, y, h, x] = v[:, 128:256]
            return carry

        lax.fori_loop(0, 4, step, 0)

    live = {}

    def first_start(h):
        for k in range(2):
            a = place[k][0]
            for e, step in ((0, 1), (1, 3)):
                cp = copy(
                    part.at[k, (a + 2) % 4, h, pl.ds(2 * e, 2)], r1.at[k, h, e],
                    rs1_s.at[k, h, e], rs1_r.at[k, h, e], {"bricks": moved(b, way[k][0], 4, step)},
                )
                cp.start()
                live[1, k, h, e] = cp

    def second_start(h):
        for k in range(2):
            a = place[k][0]
            for e, step in ((0, 1), (1, 3)):
                live[1, k, h, e].wait()
                to = (a + step) % 4
                part[k, to, h, pl.ds(2 * e, 2)] += r1[k, h, e]
                cp = copy(
                    part.at[k, to, h], r2.at[k, h, e], rs2_s.at[k, h, e], rs2_r.at[k, h, e],
                    {"bricks": moved(b, way[k][0], 4, step)},
                )
                cp.start()
                live[2, k, h, e] = cp

    def third_start(h):
        for k in range(2):
            a, at = place[k]
            for e in range(2):
                live[2, k, h, e].wait()
            part[k, a, h] += r2[k, h, 0] + r2[k, h, 1]
            for j in range(1, 4):
                cp = copy(
                    part.at[k, a, h, (at + j) % 4], r3.at[k, h, j - 1], rs3_s.at[k, h, j - 1], rs3_r.at[k, h, j - 1],
                    {"bricks": moved(b, way[k][1], 4, j)},
                )
                cp.start()
                live[3, k, h, j] = cp

    def third_end(h):
        for k in range(2):
            a, at = place[k]
            for j in range(1, 4):
                live[3, k, h, j].wait()
            part[k, a, h, at] += r3[k, h, 0] + r3[k, h, 1] + r3[k, h, 2]

    def fourth_start():
        for k in range(2):
            a, at = place[k]
            for j in range(1, 4):
                cp = copy(
                    part.at[k, a, (hm + j) % 4, at], r4.at[k, j - 1], rs4_s.at[k, j - 1], rs4_r.at[k, j - 1],
                    {"bricks": moved(b, 32, 4, j)},
                )
                cp.start()
                live[4, k, j] = cp

    def fourth_end():
        for k in range(2):
            a, at = place[k]
            for j in range(1, 4):
                live[4, k, j].wait()
            fin[:, pl.ds(128 * k, 128)] = part[k, a, hm, at] + r4[k, 0] + r4[k, 1] + r4[k, 2]

    for h in range(4):
        taps(CUTS[h], CUTS[h + 1])
        deal(h)
        first_start(h)
        if h >= 2:
            second_start(h - 2)

    conv(zz, w_back, acc_b, 5, 9)
    second_start(2)

    def slot_block(j, plane):
        at = pl.ds(pl.multiple_of(256 * c + 64 * plane, 64), 64)
        return at, activation(fs[j, at, :], conds[j])

    def back_pass(plane, carry):
        one, two = carry
        for j in range(4):
            at, (m, f, apart, pre, sigma) = slot_block(j, plane)
            back = acc_b[plane, cy[j], :, cz[j]].reshape(64, 256)
            sg = jnp.where(m, gamma * back * sigma * (1.0 + pre * (1.0 - sigma)), 0.0)
            sg_s[j, plane] = sg
            one = one + block_sum(sg)
            two = two + block_sum(sg * (apart * inv_std))
        return one, two

    zero = jnp.zeros((8, 256), F32)
    one, two = lax.fori_loop(0, 4, back_pass, (zero, zero))
    own[3] = packet(column_sum(one), column_sum(two))
    sent = spread_start(3, 1, 8, back1, 13)
    second_start(3)
    conv(hz, w_fwd, acc_f, 0, 3)
    own[4] = sum(spread_end(sent, 3, back1))
    sent = spread_start(4, 8, 4, back2, 20)
    third_start(0)
    conv(hz, w_fwd, acc_f, 3, 6)
    own[5] = sum(spread_end(sent, 4, back2))
    sent = spread_start(5, 32, 4, back3, 23)
    third_start(1)
    conv(hz, w_fwd, acc_f, 6, 9)
    third_start(2)

    def out_pass(plane, carry):
        for j in range(4):
            at = pl.ds(pl.multiple_of(256 * c + 64 * plane, 64), 64)
            f = fs[j, at, :].astype(F32)
            made = acc_f[plane, cy[j], :, cz[j]].reshape(64, 256)
            outs[j, at, :] = jnp.where(f < LIMIT, f + made, 0.0).astype(BF16)
        return carry

    lax.fori_loop(0, 4, out_pass, 0)
    theirs = pl.ds(2 - 2 * c, 2)
    half_rows = pl.ds(pl.multiple_of(256 * c, 256), 256)

    def hand_over(ref, k):
        piece = ref.at[theirs, half_rows]
        cp = copy(piece, piece, res_s.at[k], res_r.at[k], {"bricks": other})
        cp.start()
        return cp

    out_copy = hand_over(outs, 0)
    third_end(0)
    sums = sum(spread_end(sent, 5, back3))
    grad_mean = group_sum(sums[0:1]) / total_g
    cross_mean = group_sum(sums[1:2]) / total_g
    third_end(1)
    third_start(3)

    def grad_pass(plane, carry):
        for j in range(4):
            at = pl.ds(pl.multiple_of(256 * c + 64 * plane, 64), 64)
            f = fs[j, at, :].astype(F32)
            x_hat = (f - mean) * inv_std
            v = inv_std * (sg_s[j, plane] - grad_mean - x_hat * cross_mean) + zs[j, at, :].astype(F32)
            grads[j, at, :] = jnp.where(f < LIMIT, v, 0.0).astype(BF16)
        return carry

    lax.fori_loop(0, 4, grad_pass, 0)
    grad_copy = hand_over(grads, 1)
    third_end(2)
    third_end(3)
    fourth_start()
    out_copy.wait()
    out[...] = outs[mine]
    grad_copy.wait()
    fgrad[...] = grads[mine]
    fourth_end()
    clique = [{"dp": 1 - d, "bricks": b}, {"dp": 1 - d, "bricks": other}, {"bricks": other}]
    last = []
    for k, dev in enumerate(clique):
        cp = copy(fin, fin_r.at[k], fin_s.at[k], fin_rs.at[k], dev)
        cp.start()
        last.append(cp)
    for cp in edge_copies:
        cp.wait_send()
    for cp in last:
        cp.wait()
    whole = jnp.where(c == d, fin[...] + fin_r[0], fin_r[1] + fin_r[2])
    wgrad[...] = jnp.where(c == 0, whole[0:27], whole[27:54])


def on_device(features, active, neighbours, cond, gamma, beta, weight, cotangent):
    vmem = pl.BlockSpec(memory_space=pltpu.VMEM)
    dma = pltpu.SemaphoreType.DMA
    scratch = [
        pltpu.VMEM((5, 512, 256), BF16),
        pltpu.VMEM((5, 512, 256), BF16),
        pltpu.VMEM((5, 64, 256), BF16),
        pltpu.VMEM((5, 64, 256), BF16),
        pltpu.VMEM((5, 8, 256), F32),
        pltpu.VMEM((5, 8, 256), F32),
        pltpu.VMEM((2, 8, 128), jnp.int32),
        pltpu.SMEM((2, 8, 128), jnp.int32),
        pltpu.VMEM((9, 768, 256), BF16),
        pltpu.VMEM((9, 768, 256), BF16),
        pltpu.VMEM((10, 288, 768), BF16),
        pltpu.VMEM((10, 288, 768), BF16),
        pltpu.VMEM((256, 2048), BF16),
        pltpu.VMEM((ROWS + 256, 256), F32),
        pltpu.VMEM((2, 4, 4, 4, 56, 128), F32),
        pltpu.VMEM((2, 4, 2, 2, 56, 128), F32),
        pltpu.VMEM((2, 4, 2, 4, 56, 128), F32),
        pltpu.VMEM((2, 4, 3, 56, 128), F32),
        pltpu.VMEM((2, 3, 56, 128), F32),
        pltpu.VMEM((56, 256), F32),
        pltpu.VMEM((3, 56, 256), F32),
        pltpu.VMEM((4, 2, 8, 2, 8, 256), F32),
        pltpu.VMEM((4, 2, 8, 2, 8, 256), F32),
        pltpu.VMEM((4, 4, 64, 256), F32),
        pltpu.VMEM((4, 512, 256), BF16),
        pltpu.VMEM((4, 512, 256), BF16),
        pltpu.VMEM((6, 8, 256), F32),
        pltpu.VMEM((7, 8, 256), F32),
        pltpu.VMEM((3, 8, 256), F32),
        pltpu.VMEM((3, 8, 256), F32),
        pltpu.VMEM((7, 8, 256), F32),
        pltpu.VMEM((3, 8, 256), F32),
        pltpu.VMEM((3, 8, 256), F32),
        dma, dma, dma((4,)), dma((4,)), dma((6,)), dma((3, 2)), dma((26,)), dma((26,)),
        dma((2, 4, 2)), dma((2, 4, 2)), dma((2, 4, 2)), dma((2, 4, 2)),
        dma((2, 4, 3)), dma((2, 4, 3)), dma((2, 3)), dma((2, 3)),
        dma((3,)), dma((3,)), dma((2,)), dma((2,)),
    ]
    output, feature_grad, weight_grad = pl.pallas_call(
        kernel,
        out_shape=(
            jax.ShapeDtypeStruct((2, 512, 256), BF16),
            jax.ShapeDtypeStruct((2, 512, 256), BF16),
            jax.ShapeDtypeStruct((27, 256), F32),
        ),
        in_specs=[vmem] * 7 + [pl.BlockSpec(memory_space=pl.ANY)],
        out_specs=(vmem, vmem, vmem),
        scratch_shapes=scratch,
        compiler_params=pltpu.CompilerParams(
            collective_id=0, has_side_effects=True, vmem_limit_bytes=60 * 2**20
        ),
        name="layer",
    )(
        features[0], cotangent[0], active[0], neighbours[0], cond[0],
        gamma.reshape(1, 256), beta.reshape(1, 256), weight.reshape(9, 768, 256),
    )
    return output[None], feature_grad[None], weight_grad.reshape(-1)


def solution(mesh):
    whole = P("dp", "bricks", None, None)
    rows = P("dp", "bricks", None)
    return jax.shard_map(
        on_device, mesh=mesh, in_specs=(whole, rows, rows, rows, P(), P(), P(), whole),
        out_specs=(whole, whole, P(("dp", "bricks"))), check_vma=False,
    )
```

time: 1390 us -> 79 us (0.06)
  the two profiles are of different devices: /device:TPU:128 before, /device:TPU:1 now
where the time goes in v1:
time: 79 us; the launch traced here: 78.7 us
  Pallas kernels  72.9 us (92%)
  local copies, waits for them, and re-layouts  5.1 us (6%)
    pallas_call x1, Pallas kernels, on_device(): pl.pallas_call(kernel, out_shape=(jax.ShapeDtypeStruct((2, 512, 256), BF1...  72.9 us
    unnamed x2, local copies, waits for them, and re-layouts  3.73 us

profile of v1, /device:TPU:1, one launch (start us, length us, event | category | flops | bytes accessed | tf_op | source)
XLA Modules:
  0.0 78.7 jit_solution(14998143122759201215)
XLA Ops:
  0.6 72.9 %layer.1 = (bf16[2,512,256]{2,1,0:T(8,128)(2,1)}, bf16[2,512,256]{2,1,0:T(8,128)(2,1)}, f32[27,256]{1,0:T(8,128)}) custom-call(bf16[2,512,256]{2,1,0:T(8,128)(2,1)} %bitcast.11, bf16[2,512,256]{2,1,0:T(8,128)(2,1)} %bitcast.12, s32[2,512]{1,0:T(2,128)} %bitcast.15, s32[2,27]{1,0:T(2,128)} %bitcast.16, bf16[2,256]{1,0:T(2,128)(2,1)} %bitcast.17, ...), custom_call_target="tpu_custom_call" | custom-call | tf_op jit(solution)/shard_map/layer/pallas_call | solution.py:547
  73.6 1.4 %reshape.21 = f32[6912]{0:T(1024)} reshape(f32[27,256]{1,0:T(8,128)} %get-tuple-element.8) | data formatting | bytes 55296 | tf_op jit(solution)/shard_map/reshape | solution.py:565
  74.9 1.9 %copy.13 = bf16[1,2,512,256]{3,2,1,0:T(8,128)(2,1)} copy(bf16[1,2,512,256]{3,2,1,0:T(8,128)(2,1)} %bitcast.14) | data formatting | bytes 1048576
  76.8 1.9 %copy.14 = bf16[1,2,512,256]{3,2,1,0:T(8,128)(2,1)} copy(bf16[1,2,512,256]{3,2,1,0:T(8,128)(2,1)} %bitcast.13) | data formatting | bytes 1048576

commit v2 on v1

--- a/solution.py
+++ b/solution.py
@@ -61,14 +61,14 @@
 
 
 def kernel(
-    feat, cot, act, nbr, cond, gamma_in, beta_in, w_hbm,
+    feat_hbm, cot_hbm, act, nbr, cond, gamma_in, beta_in, w_hbm,
     out, fgrad, wgrad,
-    fs, zs, face_f, face_z, conds, conds_e, nbv, nbs,
-    w_fwd, w_back, hz, zz, zt, wg, part, r1, r2, r3, r4, fin, fin_r,
+    feat, cot, fs, zs, face_f, face_z, conds, conds_e, nbv, nbs,
+    w_fwd, w_back, hz, zz, zt, wg, part, r1, r2, r3, zr,
     acc_f, acc_b, sg_s, outs, grads,
-    own, got1, got2, got3, back1, back2, back3,
-    w_sem, nb_sem, core_s, core_r, edge_s, edge_r, st_s, st_r, rs1_s, rs1_r, rs2_s, rs2_r, rs3_s, rs3_r, rs4_s, rs4_r,
-    fin_s, fin_rs, res_s, res_r,
+    own, got1, got2, back1, back2,
+    w_sem, nb_sem, core_s, core_r, edge_s, edge_r, st_s, st_r, rs1_s, rs1_r, rs2_s, rs2_r, rs3_s, rs3_r, z_s, z_r,
+    res_s, res_r, in_sem, out_sem,
 ):
     d = lax.axis_index("dp")
     b = lax.axis_index("bricks")
@@ -87,14 +87,25 @@
             src_ref=src, dst_ref=dst, send_sem=ssem, recv_sem=rsem, device_id=dev, device_id_type=MESH
         )
 
+    in_copies = []
+    for s in range(2):
+        for k, (src, dst) in enumerate(((feat_hbm, feat), (cot_hbm, cot))):
+            cp = pltpu.make_async_copy(src.at[s], dst.at[s], in_sem.at[s, k])
+            cp.start()
+            in_copies.append(cp)
     w_copy = pltpu.make_async_copy(w_hbm, w_fwd, w_sem)
     w_copy.start()
 
     barrier = pltpu.get_barrier_semaphore()
     partners = [{"bricks": moved(b, 1, 8, j)} for j in range(1, 8)]
-    partners += [{"bricks": moved(b, 8, 4, j)} for j in range(1, 4)]
-    partners += [{"bricks": moved(b, 32, 4, j)} for j in range(1, 4)]
-    partners += [{"dp": 1 - d, "bricks": b}, {"dp": 1 - d, "bricks": other}]
+    across = [moved(moved(b, 8, 4, j), 32, 4, i) for j in range(4) for i in range(4)][1:]
+    partners += [{"bricks": dev} for dev in across[3:]]
+    for j in range(4):
+        up = moved(b, 32, 4, j)
+        flip = up + 1 - 2 * c
+        partners += [{"dp": 1 - d, "bricks": up}, {"dp": 1 - d, "bricks": flip}]
+        if j:
+            partners += [{"bricks": up}, {"bricks": flip}]
     partners += [{"bricks": after0}, {"bricks": before1}, {"bricks": beside}, {"bricks": beside + 1}]
     for dev in partners:
         pl.semaphore_signal(barrier, inc=1, device_id=dev, device_id_type=MESH)
@@ -105,6 +116,8 @@
     flags_t = flags.T
     first = jnp.zeros((8, 256), F32)
     for s in range(2):
+        in_copies[2 * s].wait()
+        in_copies[2 * s + 1].wait()
         for j in range(4):
             at = pl.ds(128 * j, 128)
             m = jnp.broadcast_to(flags_t[:, 4 * s + j : 4 * s + j + 1], (128, 256)) > 0.5
@@ -129,13 +142,10 @@
         conds[2 * c + s] = jnp.broadcast_to(cond[s : s + 1, :].astype(F32), (8, 256))
     pl.semaphore_wait(barrier, len(partners))
 
-    def spread_start(stage, stride, size, boxes, base):
+    def spread_start(stage, devices, boxes, base):
         sent = []
-        for j in range(1, size):
-            cp = copy(
-                own.at[stage], boxes.at[j - 1], st_s.at[base + j - 1], st_r.at[base + j - 1],
-                {"bricks": moved(b, stride, size, j)},
-            )
+        for j, dev in enumerate(devices):
+            cp = copy(own.at[stage], boxes.at[j], st_s.at[base + j], st_r.at[base + j], {"bricks": dev})
             cp.start()
             sent.append(cp)
         return sent
@@ -145,7 +155,8 @@
             cp.wait()
         return [own[stage]] + [boxes[j] for j in range(len(sent))]
 
-    sent = spread_start(0, 1, 8, got1, 0)
+    near = [moved(b, 1, 8, j) for j in range(1, 8)]
+    sent = spread_start(0, near, got1, 0)
 
     mine = pl.ds(2 * c, 2)
     core_copies = [
@@ -194,7 +205,7 @@
 
     merged = pooled(spread_end(sent, 0, got1))
     own[1] = merged
-    sent = spread_start(1, 8, 4, got2, 7)
+    sent = spread_start(1, across, got2, 7)
 
     core_copies[0].wait()
     nb_copy = pltpu.make_async_copy(nbv, nbs, nb_sem)
@@ -250,10 +261,6 @@
     for half in range(2):
         lay(zz, edge_plane, half, joined(*[face_z[src_e[2 * half + e]].astype(F32) for e in range(2)]))
 
-    merged = pooled(spread_end(sent, 1, got2))
-    own[2] = merged
-    sent = spread_start(2, 32, 4, got3, 10)
-
     def conv(grid, taps, acc, low, high):
         def step(g, carry):
             at = pl.ds(pl.multiple_of((g % 3) * 16, 16), 256)
@@ -265,9 +272,9 @@
 
     acc_f[...] = jnp.zeros(acc_f.shape, F32)
     acc_b[...] = jnp.zeros(acc_b.shape, F32)
-    conv(zz, w_back, acc_b, 0, 5)
-
-    merged = pooled(spread_end(sent, 2, got3))
+    conv(zz, w_back, acc_b, 0, 9)
+
+    merged = pooled(spread_end(sent, 1, got2))
     total = merged[2:3]
     first, second = merged[0:1], merged[1:2]
     total_g = 8.0 * total
@@ -377,30 +384,65 @@
                 cp.start()
                 live[3, k, h, j] = cp
 
-    def third_end(h):
+    side = jnp.where(c == d, 0, 1)
+
+    def window(core):
+        return pl.ds(pl.multiple_of(24 * core, 8), 32)
+
+    def to_self(h):
+        return (c == d) & (hm == h)
+
+    def z_copies(h):
+        one, two = [], []
+        for k in range(2):
+            a, at = place[k]
+            base = b % 32 + 32 * h
+            for group, core, dev in ((one, 1 - c, base + 1 - 2 * c), (two, c, base)):
+                group.append(copy(
+                    part.at[k, a, h, at, window(core)], zr.at[side, hm, k],
+                    z_s.at[h, len(group), k], z_r.at[side, hm, k], {"dp": c, "bricks": dev},
+                ))
+        return one, two
+
+    def z_start(h):
         for k in range(2):
             a, at = place[k]
             for j in range(1, 4):
                 live[3, k, h, j].wait()
             part[k, a, h, at] += r3[k, h, 0] + r3[k, h, 1] + r3[k, h, 2]
-
-    def fourth_start():
+        one, two = z_copies(h)
+        for cp in one:
+            cp.start()
+
+        @pl.when(jnp.logical_not(to_self(h)))
+        def _():
+            for cp in two:
+                cp.start()
+
+        @pl.when(to_self(h))
+        def _():
+            for k in range(2):
+                a, at = place[k]
+                zr[0, h, k] = part[k, a, h, at, window(c), :]
+
+    def z_end():
+        for h in range(4):
+            one, two = z_copies(h)
+            for cp in one:
+                cp.wait_send()
+
+            @pl.when(jnp.logical_not(to_self(h)))
+            def _():
+                for cp in two:
+                    cp.wait_send()
+                for k in range(2):
+                    copy(zr.at[0, h, k], zr.at[0, h, k], z_s.at[h, 0, k], z_r.at[0, h, k], {"bricks": other}).wait_recv()
+
+            for k in range(2):
+                copy(zr.at[1, h, k], zr.at[1, h, k], z_s.at[h, 0, k], z_r.at[1, h, k], {"bricks": other}).wait_recv()
         for k in range(2):
-            a, at = place[k]
-            for j in range(1, 4):
-                cp = copy(
-                    part.at[k, a, (hm + j) % 4, at], r4.at[k, j - 1], rs4_s.at[k, j - 1], rs4_r.at[k, j - 1],
-                    {"bricks": moved(b, 32, 4, j)},
-                )
-                cp.start()
-                live[4, k, j] = cp
-
-    def fourth_end():
-        for k in range(2):
-            a, at = place[k]
-            for j in range(1, 4):
-                live[4, k, j].wait()
-            fin[:, pl.ds(128 * k, 128)] = part[k, a, hm, at] + r4[k, 0] + r4[k, 1] + r4[k, 2]
+            v = sum(zr[e, h, k] for e in range(2) for h in range(4))
+            wgrad[pl.ds(k, 27, stride=2), :] = jnp.where(c == 0, v[0:27], v[3:30])
 
     for h in range(4):
         taps(CUTS[h], CUTS[h + 1])
@@ -408,9 +450,6 @@
         first_start(h)
         if h >= 2:
             second_start(h - 2)
-
-    conv(zz, w_back, acc_b, 5, 9)
-    second_start(2)
 
     def slot_block(j, plane):
         at = pl.ds(pl.multiple_of(256 * c + 64 * plane, 64), 64)
@@ -429,17 +468,18 @@
 
     zero = jnp.zeros((8, 256), F32)
     one, two = lax.fori_loop(0, 4, back_pass, (zero, zero))
-    own[3] = packet(column_sum(one), column_sum(two))
-    sent = spread_start(3, 1, 8, back1, 13)
+    own[2] = packet(column_sum(one), column_sum(two))
+    sent = spread_start(2, near, back1, 22)
+    second_start(2)
+    conv(hz, w_fwd, acc_f, 0, 2)
     second_start(3)
-    conv(hz, w_fwd, acc_f, 0, 3)
-    own[4] = sum(spread_end(sent, 3, back1))
-    sent = spread_start(4, 8, 4, back2, 20)
     third_start(0)
-    conv(hz, w_fwd, acc_f, 3, 6)
-    own[5] = sum(spread_end(sent, 4, back2))
-    sent = spread_start(5, 32, 4, back3, 23)
+    conv(hz, w_fwd, acc_f, 2, 4)
+    own[3] = sum(spread_end(sent, 2, back1))
+    sent = spread_start(3, across, back2, 29)
     third_start(1)
+    conv(hz, w_fwd, acc_f, 4, 6)
+    z_start(0)
     conv(hz, w_fwd, acc_f, 6, 9)
     third_start(2)
 
@@ -462,12 +502,10 @@
         return cp
 
     out_copy = hand_over(outs, 0)
-    third_end(0)
-    sums = sum(spread_end(sent, 5, back3))
+    z_start(1)
+    sums = sum(spread_end(sent, 3, back2))
     grad_mean = group_sum(sums[0:1]) / total_g
     cross_mean = group_sum(sums[1:2]) / total_g
-    third_end(1)
-    third_start(3)
 
     def grad_pass(plane, carry):
         for j in range(4):
@@ -480,32 +518,48 @@
 
     lax.fori_loop(0, 4, grad_pass, 0)
     grad_copy = hand_over(grads, 1)
-    third_end(2)
-    third_end(3)
-    fourth_start()
+    third_start(3)
     out_copy.wait()
-    out[...] = outs[mine]
+    stores = [pltpu.make_async_copy(outs.at[mine], out, out_sem.at[0])]
+    stores[0].start()
+    z_start(2)
     grad_copy.wait()
-    fgrad[...] = grads[mine]
-    fourth_end()
-    clique = [{"dp": 1 - d, "bricks": b}, {"dp": 1 - d, "bricks": other}, {"bricks": other}]
-    last = []
-    for k, dev in enumerate(clique):
-        cp = copy(fin, fin_r.at[k], fin_s.at[k], fin_rs.at[k], dev)
-        cp.start()
-        last.append(cp)
+    stores.append(pltpu.make_async_copy(grads.at[mine], fgrad, out_sem.at[1]))
+    stores[1].start()
+    z_start(3)
     for cp in edge_copies:
         cp.wait_send()
-    for cp in last:
+    for cp in stores:
         cp.wait()
-    whole = jnp.where(c == d, fin[...] + fin_r[0], fin_r[1] + fin_r[2])
-    wgrad[...] = jnp.where(c == 0, whole[0:27], whole[27:54])
+    z_end()
+
+
+def hand_out(*refs):
+    sources, targets, held, sem_in, sem_out = refs[:3], refs[3:6], refs[6:9], refs[9], refs[10]
+    steps = []
+    for i in range(3):
+        rows = sources[i].shape[0]
+        for k in range(1 if i == 2 else rows):
+            at = pl.ds(0, rows) if i == 2 else pl.ds(k, 1)
+            steps.append((
+                pltpu.make_async_copy(sources[i].at[at], held[i].at[at], sem_in.at[i, k]),
+                pltpu.make_async_copy(held[i].at[at], targets[i].at[at], sem_out.at[i, k]),
+            ))
+    for load, _ in steps:
+        load.start()
+    for load, store in steps:
+        load.wait()
+        store.start()
+    for _, store in steps:
+        store.wait()
 
 
 def on_device(features, active, neighbours, cond, gamma, beta, weight, cotangent):
     vmem = pl.BlockSpec(memory_space=pltpu.VMEM)
     dma = pltpu.SemaphoreType.DMA
     scratch = [
+        pltpu.VMEM((2, 512, 256), BF16),
+        pltpu.VMEM((2, 512, 256), BF16),
         pltpu.VMEM((5, 512, 256), BF16),
         pltpu.VMEM((5, 512, 256), BF16),
         pltpu.VMEM((5, 64, 256), BF16),
@@ -524,35 +578,33 @@
         pltpu.VMEM((2, 4, 2, 2, 56, 128), F32),
         pltpu.VMEM((2, 4, 2, 4, 56, 128), F32),
         pltpu.VMEM((2, 4, 3, 56, 128), F32),
-        pltpu.VMEM((2, 3, 56, 128), F32),
-        pltpu.VMEM((56, 256), F32),
-        pltpu.VMEM((3, 56, 256), F32),
+        pltpu.VMEM((2, 4, 2, 32, 128), F32),
         pltpu.VMEM((4, 2, 8, 2, 8, 256), F32),
         pltpu.VMEM((4, 2, 8, 2, 8, 256), F32),
         pltpu.VMEM((4, 4, 64, 256), F32),
         pltpu.VMEM((4, 512, 256), BF16),
         pltpu.VMEM((4, 512, 256), BF16),
-        pltpu.VMEM((6, 8, 256), F32),
+        pltpu.VMEM((4, 8, 256), F32),
         pltpu.VMEM((7, 8, 256), F32),
-        pltpu.VMEM((3, 8, 256), F32),
-        pltpu.VMEM((3, 8, 256), F32),
+        pltpu.VMEM((15, 8, 256), F32),
         pltpu.VMEM((7, 8, 256), F32),
-        pltpu.VMEM((3, 8, 256), F32),
-        pltpu.VMEM((3, 8, 256), F32),
-        dma, dma, dma((4,)), dma((4,)), dma((6,)), dma((3, 2)), dma((26,)), dma((26,)),
+        pltpu.VMEM((15, 8, 256), F32),
+        dma, dma, dma((4,)), dma((4,)), dma((6,)), dma((3, 2)), dma((44,)), dma((44,)),
         dma((2, 4, 2)), dma((2, 4, 2)), dma((2, 4, 2)), dma((2, 4, 2)),
-        dma((2, 4, 3)), dma((2, 4, 3)), dma((2, 3)), dma((2, 3)),
-        dma((3,)), dma((3,)), dma((2,)), dma((2,)),
+        dma((2, 4, 3)), dma((2, 4, 3)), dma((4, 2, 2)), dma((2, 4, 2)),
+        dma((2,)), dma((2,)), dma((2, 2)), dma((2,)),
     ]
-    output, feature_grad, weight_grad = pl.pallas_call(
+    shapes = (
+        jax.ShapeDtypeStruct((2, 512, 256), BF16),
+        jax.ShapeDtypeStruct((2, 512, 256), BF16),
+        jax.ShapeDtypeStruct((54, 128), F32),
+    )
+    anywhere = pl.BlockSpec(memory_space=pl.ANY)
+    made = pl.pallas_call(
         kernel,
-        out_shape=(
-            jax.ShapeDtypeStruct((2, 512, 256), BF16),
-            jax.ShapeDtypeStruct((2, 512, 256), BF16),
-            jax.ShapeDtypeStruct((27, 256), F32),
-        ),
-        in_specs=[vmem] * 7 + [pl.BlockSpec(memory_space=pl.ANY)],
-        out_specs=(vmem, vmem, vmem),
+        out_shape=shapes,
+        in_specs=[anywhere] * 2 + [vmem] * 5 + [anywhere],
+        out_specs=(anywhere, anywhere, vmem),
         scratch_shapes=scratch,
         compiler_params=pltpu.CompilerParams(
             collective_id=0, has_side_effects=True, vmem_limit_bytes=60 * 2**20
@@ -562,6 +614,11 @@
         features[0], cotangent[0], active[0], neighbours[0], cond[0],
         gamma.reshape(1, 256), beta.reshape(1, 256), weight.reshape(9, 768, 256),
     )
+    output, feature_grad, weight_grad = pl.pallas_call(
+        hand_out, out_shape=shapes, in_specs=[anywhere] * 3, out_specs=(anywhere,) * 3,
+        scratch_shapes=[pltpu.VMEM(v.shape, v.dtype) for v in shapes] + [dma((3, 2)), dma((3, 2))],
+        compiler_params=pltpu.CompilerParams(vmem_limit_bytes=60 * 2**20), name="hand_out",
+    )(*made)
     return output[None], feature_grad[None], weight_grad.reshape(-1)
 
 

time: 79 us -> 69.4 us (0.88)
  local copies, waits for them, and re-layouts: 5.1 us -> 0 us
  Pallas kernels: 72.9 us -> 68.6 us
    pallas_call x1 -> x2, Pallas kernels: 72.9 us -> 68.6 us  [the longest x1 66.6 us: on_device(): pl.pallas_call(kernel, out_shape=shapes, in_specs=[anywhere] * 2 + [vmem]...]
    unnamed x2 -> x0, local copies, waits for them, and re-layouts: 3.73 us -> none
    reshape x1 -> x0, local copies, waits for them, and re-layouts: 1.37 us -> none  [on_device(): return (output[None], feature_grad[None], weight_grad.reshape(-1))]
where the time goes in v2:
time: 69.4 us; the launch traced here: 69.3 us
  Pallas kernels  68.6 us (99%)
    pallas_call x1, Pallas kernels, on_device(): pl.pallas_call(kernel, out_shape=shapes, in_specs=[anywhere] * 2 + [vmem]...  66.6 us
    pallas_call x1, Pallas kernels, on_device(): pl.pallas_call(hand_out, out_shape=shapes, in_specs=[anywhere] * 3, out_s...  2.02 us

profile of v2, /device:TPU:1, one launch (start us, length us, event | category | flops | bytes accessed | tf_op | source)
XLA Modules:
  0.0 69.3 jit_solution(8882096616898194112)
XLA Ops:
  0.6 66.6 %layer.1 = (bf16[2,512,256]{2,1,0:T(8,128)(2,1)}, bf16[2,512,256]{2,1,0:T(8,128)(2,1)}, f32[54,128]{1,0:T(8,128)}) custom-call(bf16[2,512,256]{2,1,0:T(8,128)(2,1)} %bitcast.12, bf16[2,512,256]{2,1,0:T(8,128)(2,1)} %bitcast.13, s32[2,512]{1,0:T(2,128)} %bitcast.14, s32[2,27]{1,0:T(2,128)} %bitcast.15, bf16[2,256]{1,0:T(2,128)(2,1)} %bitcast.16, ...), custom_call_target="tpu_custom_call" | custom-call | tf_op jit(solution)/shard_map/layer/pallas_call | solution.py:603
  67.2 2.0 %hand_out.1 = (bf16[2,512,256]{2,1,0:T(8,128)(2,1)}, bf16[2,512,256]{2,1,0:T(8,128)(2,1)}, f32[54,128]{1,0:T(8,128)}) custom-call(bf16[2,512,256]{2,1,0:T(8,128)(2,1)} %get-tuple-element.9.refs_0_, bf16[2,512,256]{2,1,0:T(8,128)(2,1)} %get-tuple-element.10.refs_1_, f32[54,128]{1,0:T(8,128)} %get-tuple-element.11.refs_2_), custom_call_target="tpu_custom_call" | custom-call | tf_op jit(solution)/shard_map/hand_out/pallas_call | solution.py:617

commit v3 on v2

--- a/solution.py
+++ b/solution.py
@@ -15,7 +15,8 @@
 LIMIT = 1e29
 LAYERS = 64
 ROWS = 3456
-CUTS = (0, 4, 8, 11, 14)
+CUTS = (0, 2, 3, 4, 5)
+LEAD = 384
 
 
 def moved(index, stride, size, step):
@@ -64,7 +65,7 @@
     feat_hbm, cot_hbm, act, nbr, cond, gamma_in, beta_in, w_hbm,
     out, fgrad, wgrad,
     feat, cot, fs, zs, face_f, face_z, conds, conds_e, nbv, nbs,
-    w_fwd, w_back, hz, zz, zt, wg, part, r1, r2, r3, zr,
+    w_fwd, w_back, hz, zz, wg, part, r1, r2, r3, zr,
     acc_f, acc_b, sg_s, outs, grads,
     own, got1, got2, back1, back2,
     w_sem, nb_sem, core_s, core_r, edge_s, edge_r, st_s, st_r, rs1_s, rs1_r, rs2_s, rs2_r, rs3_s, rs3_r, z_s, z_r,
@@ -77,7 +78,6 @@
     xm = (b // 8) % 4
     ym = (b // 2) % 4
     hm = b // 32
-    other = b + 1 - 2 * c
     after0 = ((layer + 1) % LAYERS) * 2
     before1 = ((layer + LAYERS - 1) % LAYERS) * 2 + 1
     beside = jnp.where(c == 0, (layer + LAYERS - 1) % LAYERS, (layer + 1) % LAYERS) * 2
@@ -88,24 +88,22 @@
         )
 
     in_copies = []
-    for s in range(2):
-        for k, (src, dst) in enumerate(((feat_hbm, feat), (cot_hbm, cot))):
+    for k, (src, dst) in enumerate(((feat_hbm, feat), (cot_hbm, cot))):
+        for s in range(2):
             cp = pltpu.make_async_copy(src.at[s], dst.at[s], in_sem.at[s, k])
             cp.start()
             in_copies.append(cp)
     w_copy = pltpu.make_async_copy(w_hbm, w_fwd, w_sem)
-    w_copy.start()
 
     barrier = pltpu.get_barrier_semaphore()
-    partners = [{"bricks": moved(b, 1, 8, j)} for j in range(1, 8)]
-    across = [moved(moved(b, 8, 4, j), 32, 4, i) for j in range(4) for i in range(4)][1:]
-    partners += [{"bricks": dev} for dev in across[3:]]
+    other = b + 1 - 2 * c
+    near = []
     for j in range(4):
         up = moved(b, 32, 4, j)
-        flip = up + 1 - 2 * c
-        partners += [{"dp": 1 - d, "bricks": up}, {"dp": 1 - d, "bricks": flip}]
-        if j:
-            partners += [{"bricks": up}, {"bricks": flip}]
+        near += [up, up + 1 - 2 * c]
+    across = [moved(moved(b, 8, 4, j), 2, 4, i) for j in range(4) for i in range(4)]
+    partners = [{"dp": 1 - d, "bricks": dev} for dev in near]
+    partners += [{"bricks": dev} for dev in near[1:] + across[1:]]
     partners += [{"bricks": after0}, {"bricks": before1}, {"bricks": beside}, {"bricks": beside + 1}]
     for dev in partners:
         pl.semaphore_signal(barrier, inc=1, device_id=dev, device_id_type=MESH)
@@ -114,32 +112,27 @@
     flags = jnp.concatenate(rows, axis=0).astype(F32)
     count = jnp.sum(jnp.sum(flags, axis=1, keepdims=True), axis=0, keepdims=True)
     flags_t = flags.T
+    def active_rows(s, j):
+        return jnp.broadcast_to(flags_t[:, 4 * s + j : 4 * s + j + 1], (128, 256)) > 0.5
+
+    shift = None
     first = jnp.zeros((8, 256), F32)
-    for s in range(2):
-        in_copies[2 * s].wait()
-        in_copies[2 * s + 1].wait()
-        for j in range(4):
-            at = pl.ds(128 * j, 128)
-            m = jnp.broadcast_to(flags_t[:, 4 * s + j : 4 * s + j + 1], (128, 256)) > 0.5
-            f = feat[s, at, :].astype(F32)
-            z = cot[s, at, :].astype(F32)
-            fs[2 * c + s, at, :] = jnp.where(m, f, BIG).astype(BF16)
-            zs[2 * c + s, at, :] = jnp.where(m, z, 0.0).astype(BF16)
-            first = first + block_sum(jnp.where(m, f, 0.0))
-    first = column_sum(first)
-    local_mean = first / jnp.maximum(count, 1.0)
     second = jnp.zeros((8, 256), F32)
     for s in range(2):
+        in_copies[s].wait()
         for j in range(4):
-            f = fs[2 * c + s, pl.ds(128 * j, 128), :].astype(F32)
-            apart = jnp.where(f < LIMIT, f - local_mean, 0.0)
+            m = active_rows(s, j)
+            f = feat[s, pl.ds(128 * j, 128), :].astype(F32)
+            if shift is None:
+                held = column_sum(block_sum(jnp.where(m, 1.0, 0.0)))
+                shift = column_sum(block_sum(jnp.where(m, f, 0.0))) / jnp.maximum(held, 1.0)
+            apart = jnp.where(m, f - shift, 0.0)
+            first = first + block_sum(apart)
             second = second + block_sum(apart * apart)
-    second = column_sum(second)
+    first = column_sum(first)
+    second = column_sum(second) - first * first / jnp.maximum(count, 1.0)
+    first = first + count * shift
     own[0] = packet(first, second, jnp.broadcast_to(count, (1, 256)))
-    nbv[c] = jnp.zeros((8, 128), jnp.int32)
-    nbv[c, 0:2, 0:27] = nbr[...]
-    for s in range(2):
-        conds[2 * c + s] = jnp.broadcast_to(cond[s : s + 1, :].astype(F32), (8, 256))
     pl.semaphore_wait(barrier, len(partners))
 
     def spread_start(stage, devices, boxes, base):
@@ -155,9 +148,21 @@
             cp.wait()
         return [own[stage]] + [boxes[j] for j in range(len(sent))]
 
-    near = [moved(b, 1, 8, j) for j in range(1, 8)]
-    sent = spread_start(0, near, got1, 0)
-
+    sent = spread_start(0, near[1:], got1, 0)
+
+    in_copies[2].wait()
+    in_copies[3].wait()
+    w_copy.start()
+    for s in range(2):
+        for j in range(4):
+            at = pl.ds(128 * j, 128)
+            m = active_rows(s, j)
+            fs[2 * c + s, at, :] = jnp.where(m, feat[s, at, :].astype(F32), BIG).astype(BF16)
+            zs[2 * c + s, at, :] = jnp.where(m, cot[s, at, :].astype(F32), 0.0).astype(BF16)
+    nbv[c] = jnp.zeros((8, 128), jnp.int32)
+    nbv[c, 0:2, 0:27] = nbr[...]
+    for s in range(2):
+        conds[2 * c + s] = jnp.broadcast_to(cond[s : s + 1, :].astype(F32), (8, 256))
     mine = pl.ds(2 * c, 2)
     core_copies = [
         copy(r.at[i], r.at[i], core_s.at[k], core_r.at[k], {"bricks": other})
@@ -192,7 +197,7 @@
     face_z[4] = jnp.zeros((64, 256), BF16)
     conds[4] = jnp.zeros((8, 256), F32)
     conds_e[4] = jnp.zeros((8, 256), F32)
-    wg[pl.ds(128 + ROWS, 128), :] = jnp.zeros((128, 256), F32)
+    wg[pl.ds(LEAD + ROWS, 8), :] = jnp.zeros((8, 256), F32)
 
     w_copy.wait()
 
@@ -202,10 +207,6 @@
         return carry
 
     lax.fori_loop(0, 9, turn, 0)
-
-    merged = pooled(spread_end(sent, 0, got1))
-    own[1] = merged
-    sent = spread_start(1, across, got2, 7)
 
     core_copies[0].wait()
     nb_copy = pltpu.make_async_copy(nbv, nbs, nb_sem)
@@ -247,32 +248,33 @@
     edge_plane = 9 * c
 
     core_copies[1].wait()
-    edge_wait(0, face_z)
 
     def lay_z(x, carry):
         for half in range(2):
             at = pl.ds(pl.multiple_of(64 * x, 64), 64)
             v = joined(*[zs[src[2 * half + e], at, :].astype(F32) for e in range(2)])
             lay(zz, x + 1, half, v)
-            zt[:, pl.ds(pl.multiple_of(256 * x + 128 * half, 128), 128)] = v.T.astype(BF16)
         return carry
 
     lax.fori_loop(0, 8, lay_z, 0)
+
+    merged = pooled(spread_end(sent, 0, got1))
+    own[1] = merged
+    sent = spread_start(1, across[1:], got2, 7)
+
+    def conv(grid, taps, acc, kx):
+        planes = pl.ds(4 * c + kx, 4)
+        lhs = jnp.concatenate([grid[planes, 16 * e : 16 * e + 256, :].reshape(1024, 768) for e in range(3)], axis=1)
+        rhs = taps[3 * kx : 3 * kx + 3].reshape(2304, 256)
+        made = jnp.dot(lhs, rhs, preferred_element_type=F32).reshape(4, 2, 8, 2, 8, 256)
+        acc[...] = made if kx == 1 else acc[...] + made
+
+    conv(zz, w_back, acc_b, 1)
+    edge_wait(0, face_z)
     for half in range(2):
         lay(zz, edge_plane, half, joined(*[face_z[src_e[2 * half + e]].astype(F32) for e in range(2)]))
-
-    def conv(grid, taps, acc, low, high):
-        def step(g, carry):
-            at = pl.ds(pl.multiple_of((g % 3) * 16, 16), 256)
-            lhs = grid[pl.ds(4 * c + g // 3, 4), at, :].reshape(1024, 768)
-            acc[...] += jnp.dot(lhs, taps[g], preferred_element_type=F32).reshape(4, 2, 8, 2, 8, 256)
-            return carry
-
-        lax.fori_loop(low, high, step, 0)
-
-    acc_f[...] = jnp.zeros(acc_f.shape, F32)
-    acc_b[...] = jnp.zeros(acc_b.shape, F32)
-    conv(zz, w_back, acc_b, 0, 9)
+    conv(zz, w_back, acc_b, 0)
+    conv(zz, w_back, acc_b, 2)
 
     merged = pooled(spread_end(sent, 1, got2))
     total = merged[2:3]
@@ -318,12 +320,13 @@
 
     def taps(low, high):
         def step(i, carry):
-            t = 13 * c + i
-            at = pl.ds(pl.multiple_of((t // 3) % 3 * 16, 16), 256)
-            lanes = pl.ds(pl.multiple_of(t % 3 * 256, 256), 256)
-            rhs = hz[pl.ds(t // 9, 8), at, lanes].reshape(2048, 256)
-            made = jnp.dot(zt[...], rhs, preferred_element_type=F32)
-            wg[pl.ds(pl.multiple_of(128 * (1 - c) + 256 * i, 128), 256), :] = made.T
+            g = 4 * c + i
+            at = pl.ds(pl.multiple_of(g % 3 * 16, 16), 256)
+            lhs = hz[pl.ds(g // 3, 8), at, :].reshape(2048, 768)
+            center = zz[1:9, 16:272, 256:512].reshape(2048, 256)
+            wg[pl.ds(pl.multiple_of(LEAD * (1 - c) + 768 * i, 128), 768), :] = lax.dot_general(
+                lhs, center, (((0,), (0,)), ((), ())), preferred_element_type=F32
+            )
             return carry
 
         lax.fori_loop(low, high, step, 0)
@@ -333,7 +336,7 @@
 
     def deal(h):
         def step(x, carry):
-            base = pl.multiple_of(128 + 864 * h + 216 * x, 8)
+            base = pl.multiple_of(LEAD + 864 * h + 216 * x, 8)
             for y in range(4):
                 low = 54 * y // 8 * 8
                 v = wg[pl.ds(base + low, 64), :][54 * y - low : 54 * y - low + 56]
@@ -444,13 +447,6 @@
             v = sum(zr[e, h, k] for e in range(2) for h in range(4))
             wgrad[pl.ds(k, 27, stride=2), :] = jnp.where(c == 0, v[0:27], v[3:30])
 
-    for h in range(4):
-        taps(CUTS[h], CUTS[h + 1])
-        deal(h)
-        first_start(h)
-        if h >= 2:
-            second_start(h - 2)
-
     def slot_block(j, plane):
         at = pl.ds(pl.multiple_of(256 * c + 64 * plane, 64), 64)
         return at, activation(fs[j, at, :], conds[j])
@@ -466,22 +462,11 @@
             two = two + block_sum(sg * (apart * inv_std))
         return one, two
 
-    zero = jnp.zeros((8, 256), F32)
-    one, two = lax.fori_loop(0, 4, back_pass, (zero, zero))
-    own[2] = packet(column_sum(one), column_sum(two))
-    sent = spread_start(2, near, back1, 22)
-    second_start(2)
-    conv(hz, w_fwd, acc_f, 0, 2)
-    second_start(3)
-    third_start(0)
-    conv(hz, w_fwd, acc_f, 2, 4)
-    own[3] = sum(spread_end(sent, 2, back1))
-    sent = spread_start(3, across, back2, 29)
-    third_start(1)
-    conv(hz, w_fwd, acc_f, 4, 6)
-    z_start(0)
-    conv(hz, w_fwd, acc_f, 6, 9)
-    third_start(2)
+    def back_start():
+        zero = jnp.zeros((8, 256), F32)
+        one, two = lax.fori_loop(0, 4, back_pass, (zero, zero))
+        own[2] = packet(column_sum(one), column_sum(two))
+        return spread_start(2, across[1:], back1, 22)
 
     def out_pass(plane, carry):
         for j in range(4):
@@ -491,7 +476,6 @@
             outs[j, at, :] = jnp.where(f < LIMIT, f + made, 0.0).astype(BF16)
         return carry
 
-    lax.fori_loop(0, 4, out_pass, 0)
     theirs = pl.ds(2 - 2 * c, 2)
     half_rows = pl.ds(pl.multiple_of(256 * c, 256), 256)
 
@@ -501,13 +485,7 @@
         cp.start()
         return cp
 
-    out_copy = hand_over(outs, 0)
-    z_start(1)
-    sums = sum(spread_end(sent, 3, back2))
-    grad_mean = group_sum(sums[0:1]) / total_g
-    cross_mean = group_sum(sums[1:2]) / total_g
-
-    def grad_pass(plane, carry):
+    def grad_pass(grad_mean, cross_mean, plane, carry):
         for j in range(4):
             at = pl.ds(pl.multiple_of(256 * c + 64 * plane, 64), 64)
             f = fs[j, at, :].astype(F32)
@@ -516,16 +494,39 @@
             grads[j, at, :] = jnp.where(f < LIMIT, v, 0.0).astype(BF16)
         return carry
 
-    lax.fori_loop(0, 4, grad_pass, 0)
+    for h in range(4):
+        taps(CUTS[h], CUTS[h + 1])
+        deal(h)
+        first_start(h)
+        if h == 0:
+            sent = back_start()
+        if h >= 1:
+            second_start(h - 1)
+    own[3] = sum(spread_end(sent, 2, back1))
+    sent = spread_start(3, near[1:], back2, 37)
+    conv(hz, w_fwd, acc_f, 1)
+    second_start(3)
+    third_start(0)
+    conv(hz, w_fwd, acc_f, 0)
+    third_start(1)
+    sums = sum(spread_end(sent, 3, back2))
+    grad_mean = group_sum(sums[0:1]) / total_g
+    cross_mean = group_sum(sums[1:2]) / total_g
+    lax.fori_loop(0, 4, functools.partial(grad_pass, grad_mean, cross_mean), 0)
     grad_copy = hand_over(grads, 1)
+    third_start(2)
+    conv(hz, w_fwd, acc_f, 2)
+    lax.fori_loop(0, 4, out_pass, 0)
+    out_copy = hand_over(outs, 0)
     third_start(3)
-    out_copy.wait()
-    stores = [pltpu.make_async_copy(outs.at[mine], out, out_sem.at[0])]
-    stores[0].start()
+    z_start(0)
+    z_start(1)
     z_start(2)
-    grad_copy.wait()
-    stores.append(pltpu.make_async_copy(grads.at[mine], fgrad, out_sem.at[1]))
-    stores[1].start()
+    stores = []
+    for k, (cp, ref, to) in enumerate(((out_copy, outs, out), (grad_copy, grads, fgrad))):
+        cp.wait()
+        stores.append(pltpu.make_async_copy(ref.at[mine], to, out_sem.at[k]))
+        stores[k].start()
     z_start(3)
     for cp in edge_copies:
         cp.wait_send()
@@ -572,8 +573,7 @@
         pltpu.VMEM((9, 768, 256), BF16),
         pltpu.VMEM((10, 288, 768), BF16),
         pltpu.VMEM((10, 288, 768), BF16),
-        pltpu.VMEM((256, 2048), BF16),
-        pltpu.VMEM((ROWS + 256, 256), F32),
+        pltpu.VMEM((LEAD + 3840, 256), F32),
         pltpu.VMEM((2, 4, 4, 4, 56, 128), F32),
         pltpu.VMEM((2, 4, 2, 2, 56, 128), F32),
         pltpu.VMEM((2, 4, 2, 4, 56, 128), F32),
@@ -587,8 +587,8 @@
         pltpu.VMEM((4, 8, 256), F32),
         pltpu.VMEM((7, 8, 256), F32),
         pltpu.VMEM((15, 8, 256), F32),
+        pltpu.VMEM((15, 8, 256), F32),
         pltpu.VMEM((7, 8, 256), F32),
-        pltpu.VMEM((15, 8, 256), F32),
         dma, dma, dma((4,)), dma((4,)), dma((6,)), dma((3, 2)), dma((44,)), dma((44,)),
         dma((2, 4, 2)), dma((2, 4, 2)), dma((2, 4, 2)), dma((2, 4, 2)),
         dma((2, 4, 3)), dma((2, 4, 3)), dma((4, 2, 2)), dma((2, 4, 2)),

time: 69.4 us -> 63.2 us (0.911)
  Pallas kernels: 68.6 us -> 62 us
    pallas_call x1, Pallas kernels: 66.6 us -> 59.9 us  [on_device(): pl.pallas_call(kernel, out_shape=shapes, in_specs=[anywhere] * 2 + [vmem]...]
where the time goes in v3:
time: 63.2 us; the launch traced here: 62.6 us
  Pallas kernels  62 us (98%)
  between operations  0.64 us (1%)
    pallas_call x1, Pallas kernels, on_device(): pl.pallas_call(kernel, out_shape=shapes, in_specs=[anywhere] * 2 + [vmem]...  59.9 us
    pallas_call x1, Pallas kernels, on_device(): pl.pallas_call(hand_out, out_shape=shapes, in_specs=[anywhere] * 3, out_s...  2.02 us

profile of v3, /device:TPU:1, one launch (start us, length us, event | category | flops | bytes accessed | tf_op | source)
XLA Modules:
  0.0 62.6 jit_solution(778006878407229716)
XLA Ops:
  0.6 59.9 %layer.1 = (bf16[2,512,256]{2,1,0:T(8,128)(2,1)}, bf16[2,512,256]{2,1,0:T(8,128)(2,1)}, f32[54,128]{1,0:T(8,128)}) custom-call(bf16[2,512,256]{2,1,0:T(8,128)(2,1)} %bitcast.12, bf16[2,512,256]{2,1,0:T(8,128)(2,1)} %bitcast.13, s32[2,512]{1,0:T(2,128)} %bitcast.14, s32[2,27]{1,0:T(2,128)} %bitcast.15, bf16[2,256]{1,0:T(2,128)(2,1)} %bitcast.16, ...), custom_call_target="tpu_custom_call" | custom-call | tf_op jit(solution)/shard_map/layer/pallas_call | solution.py:603
  60.6 2.0 %hand_out.1 = (bf16[2,512,256]{2,1,0:T(8,128)(2,1)}, bf16[2,512,256]{2,1,0:T(8,128)(2,1)}, f32[54,128]{1,0:T(8,128)}) custom-call(bf16[2,512,256]{2,1,0:T(8,128)(2,1)} %get-tuple-element.9.refs_0_, bf16[2,512,256]{2,1,0:T(8,128)(2,1)} %get-tuple-element.10.refs_1_, f32[54,128]{1,0:T(8,128)} %get-tuple-element.11.refs_2_), custom_call_target="tpu_custom_call" | custom-call | tf_op jit(solution)/shard_map/hand_out/pallas_call | solution.py:617

commit v4 on v3

--- a/solution.py
+++ b/solution.py
@@ -339,7 +339,7 @@
             base = pl.multiple_of(LEAD + 864 * h + 216 * x, 8)
             for y in range(4):
                 low = 54 * y // 8 * 8
-                v = wg[pl.ds(base + low, 64), :][54 * y - low : 54 * y - low + 56]
+                v = wg[pl.ds(base + low, 64), :][54 * y - low : 54 * y - low + 54]
                 part[0, x, h, y] = v[:, 0:128]
                 part[1, y, h, x] = v[:, 128:256]
             return carry
@@ -390,7 +390,7 @@
     side = jnp.where(c == d, 0, 1)
 
     def window(core):
-        return pl.ds(pl.multiple_of(24 * core, 8), 32)
+        return pl.ds(pl.multiple_of(24 * core, 8), 30)
 
     def to_self(h):
         return (c == d) & (hm == h)
@@ -518,8 +518,8 @@
     conv(hz, w_fwd, acc_f, 2)
     lax.fori_loop(0, 4, out_pass, 0)
     out_copy = hand_over(outs, 0)
+    z_start(0)
     third_start(3)
-    z_start(0)
     z_start(1)
     z_start(2)
     stores = []
@@ -574,11 +574,11 @@
         pltpu.VMEM((10, 288, 768), BF16),
         pltpu.VMEM((10, 288, 768), BF16),
         pltpu.VMEM((LEAD + 3840, 256), F32),
-        pltpu.VMEM((2, 4, 4, 4, 56, 128), F32),
-        pltpu.VMEM((2, 4, 2, 2, 56, 128), F32),
-        pltpu.VMEM((2, 4, 2, 4, 56, 128), F32),
-        pltpu.VMEM((2, 4, 3, 56, 128), F32),
-        pltpu.VMEM((2, 4, 2, 32, 128), F32),
+        pltpu.VMEM((2, 4, 4, 4, 54, 128), F32),
+        pltpu.VMEM((2, 4, 2, 2, 54, 128), F32),
+        pltpu.VMEM((2, 4, 2, 4, 54, 128), F32),
+        pltpu.VMEM((2, 4, 3, 54, 128), F32),
+        pltpu.VMEM((2, 4, 2, 30, 128), F32),
         pltpu.VMEM((4, 2, 8, 2, 8, 256), F32),
         pltpu.VMEM((4, 2, 8, 2, 8, 256), F32),
         pltpu.VMEM((4, 4, 64, 256), F32),

time: 63.2 us -> 62.1 us (0.983)
  Pallas kernels: 62 us -> 61.3 us
    pallas_call x1, Pallas kernels: 59.9 us -> 59.3 us  [on_device(): pl.pallas_call(kernel, out_shape=shapes, in_specs=[anywhere] * 2 + [vmem]...]
where the time goes in v4:
time: 62.1 us; the launch traced here: 61.9 us
  Pallas kernels  61.3 us (99%)
  between operations  0.64 us (1%)
    pallas_call x1, Pallas kernels, on_device(): pl.pallas_call(kernel, out_shape=shapes, in_specs=[anywhere] * 2 + [vmem]...  59.3 us
    pallas_call x1, Pallas kernels, on_device(): pl.pallas_call(hand_out, out_shape=shapes, in_specs=[anywhere] * 3, out_s...  2.02 us

profile of v4, /device:TPU:1, one launch (start us, length us, event | category | flops | bytes accessed | tf_op | source)
XLA Modules:
  0.0 61.9 jit_solution(2747341406362933666)
XLA Ops:
  0.6 59.3 %layer.1 = (bf16[2,512,256]{2,1,0:T(8,128)(2,1)}, bf16[2,512,256]{2,1,0:T(8,128)(2,1)}, f32[54,128]{1,0:T(8,128)}) custom-call(bf16[2,512,256]{2,1,0:T(8,128)(2,1)} %bitcast.12, bf16[2,512,256]{2,1,0:T(8,128)(2,1)} %bitcast.13, s32[2,512]{1,0:T(2,128)} %bitcast.14, s32[2,27]{1,0:T(2,128)} %bitcast.15, bf16[2,256]{1,0:T(2,128)(2,1)} %bitcast.16, ...), custom_call_target="tpu_custom_call" | custom-call | tf_op jit(solution)/shard_map/layer/pallas_call | solution.py:603
  59.9 2.0 %hand_out.1 = (bf16[2,512,256]{2,1,0:T(8,128)(2,1)}, bf16[2,512,256]{2,1,0:T(8,128)(2,1)}, f32[54,128]{1,0:T(8,128)}) custom-call(bf16[2,512,256]{2,1,0:T(8,128)(2,1)} %get-tuple-element.9.refs_0_, bf16[2,512,256]{2,1,0:T(8,128)(2,1)} %get-tuple-element.10.refs_1_, f32[54,128]{1,0:T(8,128)} %get-tuple-element.11.refs_2_), custom_call_target="tpu_custom_call" | custom-call | tf_op jit(solution)/shard_map/hand_out/pallas_call | solution.py:617

commit v5 on v4

--- a/solution.py
+++ b/solution.py
@@ -87,12 +87,6 @@
             src_ref=src, dst_ref=dst, send_sem=ssem, recv_sem=rsem, device_id=dev, device_id_type=MESH
         )
 
-    in_copies = []
-    for k, (src, dst) in enumerate(((feat_hbm, feat), (cot_hbm, cot))):
-        for s in range(2):
-            cp = pltpu.make_async_copy(src.at[s], dst.at[s], in_sem.at[s, k])
-            cp.start()
-            in_copies.append(cp)
     w_copy = pltpu.make_async_copy(w_hbm, w_fwd, w_sem)
 
     barrier = pltpu.get_barrier_semaphore()
@@ -107,6 +101,12 @@
     partners += [{"bricks": after0}, {"bricks": before1}, {"bricks": beside}, {"bricks": beside + 1}]
     for dev in partners:
         pl.semaphore_signal(barrier, inc=1, device_id=dev, device_id_type=MESH)
+    in_copies = []
+    for k, (src, dst) in enumerate(((feat_hbm, feat), (cot_hbm, cot))):
+        for s in range(2):
+            cp = pltpu.make_async_copy(src.at[s], dst.at[s], in_sem.at[s, k])
+            cp.start()
+            in_copies.append(cp)
 
     rows = [act[s : s + 1, 128 * j : 128 * j + 128] for s in range(2) for j in range(4)]
     flags = jnp.concatenate(rows, axis=0).astype(F32)
@@ -500,25 +500,26 @@
         first_start(h)
         if h == 0:
             sent = back_start()
-        if h >= 1:
+        if 1 <= h <= 2:
             second_start(h - 1)
     own[3] = sum(spread_end(sent, 2, back1))
     sent = spread_start(3, near[1:], back2, 37)
     conv(hz, w_fwd, acc_f, 1)
-    second_start(3)
     third_start(0)
+    second_start(2)
     conv(hz, w_fwd, acc_f, 0)
     third_start(1)
+    second_start(3)
     sums = sum(spread_end(sent, 3, back2))
     grad_mean = group_sum(sums[0:1]) / total_g
     cross_mean = group_sum(sums[1:2]) / total_g
     lax.fori_loop(0, 4, functools.partial(grad_pass, grad_mean, cross_mean), 0)
     grad_copy = hand_over(grads, 1)
     third_start(2)
+    z_start(0)
     conv(hz, w_fwd, acc_f, 2)
     lax.fori_loop(0, 4, out_pass, 0)
     out_copy = hand_over(outs, 0)
-    z_start(0)
     third_start(3)
     z_start(1)
     z_start(2)

time: 62.1 us -> 61.2 us (0.986)
  the two profiles are of different devices: /device:TPU:1 before, /device:TPU:192 now
where the time goes in v5:
time: 61.2 us; the launch traced here: 61 us
  Pallas kernels  60.3 us (99%)
  between operations  0.64 us (1%)
    pallas_call x1, Pallas kernels, on_device(): pl.pallas_call(kernel, out_shape=shapes, in_specs=[anywhere] * 2 + [vmem]...  58.3 us
    pallas_call x1, Pallas kernels, on_device(): pl.pallas_call(hand_out, out_shape=shapes, in_specs=[anywhere] * 3, out_s...  2.02 us

profile of v5, /device:TPU:192, one launch (start us, length us, event | category | flops | bytes accessed | tf_op | source)
XLA Modules:
  0.0 61.0 jit_solution(8674895462553526181)
XLA Ops:
  0.6 58.3 %layer.1 = (bf16[2,512,256]{2,1,0:T(8,128)(2,1)}, bf16[2,512,256]{2,1,0:T(8,128)(2,1)}, f32[54,128]{1,0:T(8,128)}) custom-call(bf16[2,512,256]{2,1,0:T(8,128)(2,1)} %bitcast.12, bf16[2,512,256]{2,1,0:T(8,128)(2,1)} %bitcast.13, s32[2,512]{1,0:T(2,128)} %bitcast.14, s32[2,27]{1,0:T(2,128)} %bitcast.15, bf16[2,256]{1,0:T(2,128)(2,1)} %bitcast.16, ...), custom_call_target="tpu_custom_call" | custom-call | tf_op jit(solution)/shard_map/layer/pallas_call | solution.py:604
  59.0 2.0 %hand_out.1 = (bf16[2,512,256]{2,1,0:T(8,128)(2,1)}, bf16[2,512,256]{2,1,0:T(8,128)(2,1)}, f32[54,128]{1,0:T(8,128)}) custom-call(bf16[2,512,256]{2,1,0:T(8,128)(2,1)} %get-tuple-element.9.refs_0_, bf16[2,512,256]{2,1,0:T(8,128)(2,1)} %get-tuple-element.10.refs_1_, f32[54,128]{1,0:T(8,128)} %get-tuple-element.11.refs_2_), custom_call_target="tpu_custom_call" | custom-call | tf_op jit(solution)/shard_map/hand_out/pallas_call | solution.py:618

commit v6 on v5

--- a/solution.py
+++ b/solution.py
@@ -510,12 +510,12 @@
     conv(hz, w_fwd, acc_f, 0)
     third_start(1)
     second_start(3)
+    third_start(2)
     sums = sum(spread_end(sent, 3, back2))
     grad_mean = group_sum(sums[0:1]) / total_g
     cross_mean = group_sum(sums[1:2]) / total_g
     lax.fori_loop(0, 4, functools.partial(grad_pass, grad_mean, cross_mean), 0)
     grad_copy = hand_over(grads, 1)
-    third_start(2)
     z_start(0)
     conv(hz, w_fwd, acc_f, 2)
     lax.fori_loop(0, 4, out_pass, 0)

time: 61.2 us -> 61.8 us (level)
  the two profiles are of different devices: /device:TPU:192 before, /device:TPU:16 now
where the time goes in v6:
time: 61.8 us; the launch traced here: 61.7 us
  Pallas kernels  61 us (99%)
  between operations  0.64 us (1%)
    pallas_call x1, Pallas kernels, on_device(): pl.pallas_call(kernel, out_shape=shapes, in_specs=[anywhere] * 2 + [vmem]...  59 us
    pallas_call x1, Pallas kernels, on_device(): pl.pallas_call(hand_out, out_shape=shapes, in_specs=[anywhere] * 3, out_s...  2.02 us

profile of v6, /device:TPU:16, one launch (start us, length us, event | category | flops | bytes accessed | tf_op | source)
XLA Modules:
  0.0 61.7 jit_solution(6873694581167753741)
XLA Ops:
  0.6 59.0 %layer.1 = (bf16[2,512,256]{2,1,0:T(8,128)(2,1)}, bf16[2,512,256]{2,1,0:T(8,128)(2,1)}, f32[54,128]{1,0:T(8,128)}) custom-call(bf16[2,512,256]{2,1,0:T(8,128)(2,1)} %bitcast.12, bf16[2,512,256]{2,1,0:T(8,128)(2,1)} %bitcast.13, s32[2,512]{1,0:T(2,128)} %bitcast.14, s32[2,27]{1,0:T(2,128)} %bitcast.15, bf16[2,256]{1,0:T(2,128)(2,1)} %bitcast.16, ...), custom_call_target="tpu_custom_call" | custom-call | tf_op jit(solution)/shard_map/layer/pallas_call | solution.py:604
  59.6 2.0 %hand_out.1 = (bf16[2,512,256]{2,1,0:T(8,128)(2,1)}, bf16[2,512,256]{2,1,0:T(8,128)(2,1)}, f32[54,128]{1,0:T(8,128)}) custom-call(bf16[2,512,256]{2,1,0:T(8,128)(2,1)} %get-tuple-element.9.refs_0_, bf16[2,512,256]{2,1,0:T(8,128)(2,1)} %get-tuple-element.10.refs_1_, f32[54,128]{1,0:T(8,128)} %get-tuple-element.11.refs_2_), custom_call_target="tpu_custom_call" | custom-call | tf_op jit(solution)/shard_map/hand_out/pallas_call | solution.py:618
